TPU v7x, 32 devices: a whole 2x2x4 slice. The times are simulated.
32 devices in a mesh: wide: 8 (over z, x), narrow: 4 (over y, core).
Axes of the slice: x: 2, y: 2, z: 4, core: 2. Of those that a mesh axis runs over, the one named last changes fastest.
Arguments:
- patches: bfloat16 [40960, 512], P(('wide', 'narrow')), may hold values from -6 to 6
- text_tokens: bfloat16 [4, 77, 512], P('narrow', None, 'wide'), may hold values from -6 to 6
- view_counts: int32 [32, 5], P(('wide', 'narrow')), may hold values from 64 to 256, as said below
- out_grad: bfloat16 [40960, 512], P(('wide', 'narrow')), may hold values from -6 to 6
- owners: int32 [12], replicated, may hold values from 0 to 3, as said below
- masters: float32 [4, 4, 512, 512], P('narrow', None, 'wide'), may hold values from -1.41421356 to 1.41421356, as said below
- first_moment: float32 [4, 4, 512, 512], P('narrow', None, 'wide'), may hold values from -541.84987 to 541.84987
- second_moment: float32 [4, 4, 512, 512], P('narrow', None, 'wide'), may hold values from 286.72 to 73728
- average: float32 [4, 4, 512, 512], P('narrow', None, 'wide'), may hold values from -1.41421356 to 1.41421356
- vec_value: float32 [4608], replicated, may hold values from -0.8 to 1.5
- vec_first: float32 [4608], replicated, may hold values from -677.3123 to 677.3123
- vec_second: float32 [4608], replicated, may hold values from 2580.48 to 114688
- vec_average: float32 [4608], replicated, may hold values from -0.8 to 1.5
Outputs:
- layer_out: bfloat16 [40960, 512], P(('wide', 'narrow'))
- patch_grad: float32 [40960, 512], P(('wide', 'narrow'))
- text_grad: float32 [4, 77, 512], P('narrow', None, 'wide')
- new_masters: float32 [4, 4, 512, 512], P('narrow', None, 'wide')
- new_first: float32 [4, 4, 512, 512], P('narrow', None, 'wide')
- new_second: float32 [4, 4, 512, 512], P('narrow', None, 'wide')
- new_average: float32 [4, 4, 512, 512], P('narrow', None, 'wide')
- new_copies: bfloat16 [4, 4, 512, 512], P('narrow', None, 'wide')
- vec_new_value: float32 [4608], replicated
- vec_new_first: float32 [4608], replicated
- vec_new_second: float32 [4608], replicated
- vec_new_average: float32 [4608], replicated
Inputs may be any that keep to these rules, and one draw needn't show every extreme that they name: `owners`: unit u is one of: query, key, value, output projection, then the 4 column blocks of the up projection, then the row blocks of the down projection. Each owner holds at most 4 units, and some owner exactly 4. `view_counts`: A view's live patches fill its first slots; every sample has a view with 256 live patches. `masters`: empty slots hold values that no output reads.
All inputs are finite; a program needn't handle non-finite values.
Results may differ from a plain program's by a relative error of at most 0.012.
The roundings to bfloat16 on the way count: a program that leaves them out, or rounds other values in their place, can miss the bound.
Values may be sent and summed in bfloat16 or wider, within the bound.
A program may use at most 192 MiB of HBM per device.

v0:
```python
import jax
import jax.numpy as jnp
from jax import lax
from jax.sharding import PartitionSpec as P

D = 512
HEADS = 8
FF = 2048
VIEWS = 5
VIEW_ROWS = 256
STEP = 5


HIGHEST = lax.Precision.HIGHEST
norm_eps = 1e-05
beta_one = 0.5
beta_two = 0.5
adam_eps = 1e-08
weight_decay = 0.1
average_keep = 0.75
vector_rate = 0.25


def matmul(left_side, right_side):
    return jnp.dot(left_side, right_side, preferred_element_type=jnp.float32)


def tmatmul(left_side, right_side):
    return lax.dot_general(
        left_side, right_side, (((0,), (0,)), ((), ())), preferred_element_type=jnp.float32
    )


def rmatmul(left_side, right_side):
    return lax.dot_general(
        left_side, right_side, (((1,), (1,)), ((), ())), preferred_element_type=jnp.float32
    )


def gelu_exact(values):
    return jax.nn.gelu(values, approximate=False)


def layer_norm(inputs, gain_vec, bias_vec):
    center = inputs - jnp.mean(inputs, axis=-1, keepdims=True)
    spread = jnp.mean(center * center, axis=-1, keepdims=True)
    return center * lax.rsqrt(spread + norm_eps) * gain_vec + bias_vec


def unit_slots(owners, narrow_count, slot_count):
    unit_ids = jnp.arange(owners.shape[0], dtype=jnp.int32)
    same_owner = owners[:, None] == owners[None, :]
    earlier = unit_ids[None, :] < unit_ids[:, None]
    unit_rank = jnp.sum((same_owner & earlier).astype(jnp.int32), axis=1)
    owner_ids = jnp.arange(narrow_count, dtype=jnp.int32)
    slot_ids = jnp.arange(slot_count, dtype=jnp.int32)
    slot_pick = (owners[None, None, :] == owner_ids[:, None, None]) & (
        unit_rank[None, None, :] == slot_ids[None, :, None]
    )
    return (unit_rank, slot_pick.astype(jnp.float32))


def unit_rates():
    blocks = FF // D
    fans = [2 * D // 3, 2 * D // 3, D, D // 64] + [D] * blocks + [FF] * blocks
    return jnp.array(fans, dtype=jnp.float32) ** (-0.5)


def split_vector(vector):
    return (
        vector[0:D],
        vector[D : 2 * D],
        vector[2 * D : 3 * D],
        vector[3 * D : 4 * D],
        vector[4 * D : 4 * D + FF],
        vector[4 * D + FF : 5 * D + FF],
    )


def adam_update(master, moment_one, moment_two, averaged, gradient, rate_value):
    moment_one = beta_one * moment_one + (1.0 - beta_one) * gradient
    moment_two = beta_two * moment_two + (1.0 - beta_two) * gradient * gradient
    mean_hat = moment_one / (1.0 - beta_one**STEP)
    second_hat = moment_two / (1.0 - beta_two**STEP)
    master = master - rate_value * (
        mean_hat / (jnp.sqrt(second_hat) + adam_eps) + weight_decay * master
    )
    averaged = average_keep * averaged + (1.0 - average_keep) * master
    return (master, moment_one, moment_two, averaged)


def local(
    patches,
    text_tokens,
    view_counts,
    out_grad,
    owners,
    masters,
    first_moment,
    second_moment,
    average,
    vec_value,
    vec_first,
    vec_second,
    vec_average,
):
    model_width = masters.shape[3]
    slot_count = masters.shape[1]
    narrow_count = lax.axis_size("narrow")
    shard_rows = model_width // lax.axis_size("wide")
    head_dim = model_width // HEADS
    score_scale = head_dim ** (-0.5)
    blocks = FF // model_width
    unit_rank, slot_pick = unit_slots(owners, narrow_count, slot_count)
    unit_count = owners.shape[0]
    own_copy = masters.astype(jnp.bfloat16)
    row_full = lax.all_gather(own_copy, "wide", axis=2, tiled=True)
    packed = lax.all_gather(row_full, "narrow", axis=0, tiled=True)
    flat_index = owners * slot_count + unit_rank
    unit_mats = jnp.take(
        packed.reshape(narrow_count * slot_count, model_width, model_width), flat_index, axis=0
    )
    w_query, w_key, w_value, w_out = (unit_mats[0], unit_mats[1], unit_mats[2], unit_mats[3])
    w_up = jnp.concatenate([unit_mats[4 + block_id] for block_id in range(blocks)], axis=1)
    w_down = jnp.concatenate(
        [unit_mats[4 + blocks + block_id] for block_id in range(blocks)], axis=0
    )
    gain_one, bias_one, gain_two, bias_two, up_bias, down_bias = split_vector(vec_value)
    text_full = lax.all_gather(text_tokens, "wide", axis=2, tiled=True)[0].astype(jnp.float32)
    positions = jnp.arange(patches.shape[0], dtype=jnp.int32)
    view_ids = positions // VIEW_ROWS
    within = positions % VIEW_ROWS
    view_match = view_ids[:, None] == jnp.arange(VIEWS, dtype=jnp.int32)[None, :]
    live_mask = jnp.any(view_match & (within[:, None] < view_counts[0][None, :]), axis=1)
    live_col = live_mask[:, None]
    inputs = patches.astype(jnp.float32)
    normed_one = layer_norm(inputs, gain_one, bias_one).astype(jnp.bfloat16)
    text_normed = layer_norm(text_full, gain_one, bias_one).astype(jnp.bfloat16)
    query = matmul(normed_one, w_query).astype(jnp.bfloat16)
    keyed = matmul(normed_one, w_key).astype(jnp.bfloat16)
    valued = matmul(normed_one, w_value).astype(jnp.bfloat16)
    text_key = matmul(text_normed, w_key).astype(jnp.bfloat16)
    text_value = matmul(text_normed, w_value).astype(jnp.bfloat16)

    def to_heads(values):
        return values.reshape(values.shape[0], HEADS, head_dim).transpose(1, 0, 2)

    def from_heads(values):
        return values.transpose(1, 0, 2).reshape(values.shape[1], model_width)

    head_args = (
        to_heads(query),
        to_heads(keyed),
        to_heads(valued),
        to_heads(text_key),
        to_heads(text_value),
    )

    def scores_for(query_head, key_head, text_key_head):
        patch_scores = jnp.where(
            live_mask[None, :], rmatmul(query_head, key_head) * score_scale, -jnp.inf
        )
        text_scores = rmatmul(query_head, text_key_head) * score_scale
        return (patch_scores, text_scores)

    def head_forward(payload):
        query_head, key_head, value_head, text_key_head, text_value_head = payload
        patch_scores, text_scores = scores_for(query_head, key_head, text_key_head)
        row_peak = jnp.maximum(jnp.max(patch_scores, axis=1), jnp.max(text_scores, axis=1))
        patch_exp = jnp.exp(patch_scores - row_peak[:, None])
        text_exp = jnp.exp(text_scores - row_peak[:, None])
        row_total = jnp.sum(patch_exp, axis=1) + jnp.sum(text_exp, axis=1)
        patch_prob = (patch_exp / row_total[:, None]).astype(jnp.bfloat16)
        text_prob = (text_exp / row_total[:, None]).astype(jnp.bfloat16)
        mixed = matmul(patch_prob, value_head) + matmul(text_prob, text_value_head)
        return (mixed.astype(jnp.bfloat16), row_peak + jnp.log(row_total))

    head_out, row_lse = lax.map(head_forward, head_args)
    attended = from_heads(head_out)
    middle = inputs + matmul(attended, w_out)
    normed_two = layer_norm(middle, gain_two, bias_two).astype(jnp.bfloat16)
    preact = matmul(normed_two, w_up) + up_bias
    active = gelu_exact(preact).astype(jnp.bfloat16)
    layer_out = jnp.where(live_col, middle + matmul(active, w_down) + down_bias, 0.0).astype(
        jnp.bfloat16
    )
    out_back = jnp.where(live_col, out_grad, jnp.zeros_like(out_grad))
    active_back = rmatmul(out_back, w_down)
    gelu_pull = jax.vjp(gelu_exact, preact)[1]
    preact_back = gelu_pull(active_back)[0].astype(jnp.bfloat16)
    normed_two_back = rmatmul(preact_back, w_up)
    norm_two_pull = jax.vjp(layer_norm, middle, gain_two, bias_two)[1]
    middle_part, gain_two_grad, bias_two_grad = norm_two_pull(normed_two_back)
    middle_back = out_back.astype(jnp.float32) + middle_part
    branch_back = middle_back.astype(jnp.bfloat16)
    attended_back = rmatmul(branch_back, w_out).astype(jnp.bfloat16)

    def head_backward(payload):
        query_head, key_head, value_head, text_key_head, text_value_head, back_head, lse_row = (
            payload
        )
        patch_scores, text_scores = scores_for(query_head, key_head, text_key_head)
        patch_prob = jnp.exp(patch_scores - lse_row[:, None])
        text_prob = jnp.exp(text_scores - lse_row[:, None])
        patch_dprob = rmatmul(back_head, value_head)
        text_dprob = rmatmul(back_head, text_value_head)
        value_grad = tmatmul(patch_prob.astype(jnp.bfloat16), back_head)
        text_value_grad = tmatmul(text_prob.astype(jnp.bfloat16), back_head)
        row_delta = jnp.sum(patch_dprob * patch_prob, axis=1) + jnp.sum(
            text_dprob * text_prob, axis=1
        )
        patch_dscore = (patch_prob * (patch_dprob - row_delta[:, None])).astype(jnp.bfloat16)
        text_dscore = (text_prob * (text_dprob - row_delta[:, None])).astype(jnp.bfloat16)
        query_grad = (
            matmul(patch_dscore, key_head) + matmul(text_dscore, text_key_head)
        ) * score_scale
        key_grad = tmatmul(patch_dscore, query_head) * score_scale
        text_key_grad = tmatmul(text_dscore, query_head) * score_scale
        return (query_grad, key_grad, value_grad, text_key_grad, text_value_grad)

    head_grads = lax.map(head_backward, head_args + (to_heads(attended_back), row_lse))
    query_back = from_heads(head_grads[0]).astype(jnp.bfloat16)
    key_back = from_heads(head_grads[1]).astype(jnp.bfloat16)
    value_back = from_heads(head_grads[2]).astype(jnp.bfloat16)
    text_key_back = from_heads(head_grads[3]).astype(jnp.bfloat16)
    text_value_back = from_heads(head_grads[4]).astype(jnp.bfloat16)
    normed_one_back = (
        rmatmul(query_back, w_query) + rmatmul(key_back, w_key) + rmatmul(value_back, w_value)
    )
    text_normed_back = rmatmul(text_key_back, w_key) + rmatmul(text_value_back, w_value)
    norm_one_pull = jax.vjp(layer_norm, inputs, gain_one, bias_one)[1]
    input_part, gain_one_grad, bias_one_grad = norm_one_pull(normed_one_back)
    patch_grad = middle_back + input_part
    text_pull = jax.vjp(layer_norm, text_full, gain_one, bias_one)[1]
    text_back, gain_text_grad, bias_text_grad = text_pull(text_normed_back)
    vector_grad = jnp.concatenate(
        [
            gain_one_grad + gain_text_grad,
            bias_one_grad + bias_text_grad,
            gain_two_grad,
            bias_two_grad,
            jnp.sum(preact_back.astype(jnp.float32), axis=0),
            jnp.sum(out_back.astype(jnp.float32), axis=0),
        ]
    )
    vector_total = lax.psum(vector_grad, ("wide", "narrow"))
    text_grad = lax.psum_scatter(text_back[None], "wide", scatter_dimension=2, tiled=True)

    def columns_of(source, offset):
        return lax.dynamic_slice_in_dim(source, offset, shard_rows * lax.axis_size("wide"), 1)

    normed_cols = columns_of(normed_one, 0)
    text_cols = columns_of(text_normed, 0)
    pieces = [
        tmatmul(normed_cols, query_back),
        tmatmul(normed_cols, key_back) + tmatmul(text_cols, text_key_back),
        tmatmul(normed_cols, value_back) + tmatmul(text_cols, text_value_back),
        tmatmul(columns_of(attended, 0), branch_back),
        tmatmul(columns_of(normed_two, 0), preact_back),
    ]
    pieces = pieces + [
        tmatmul(columns_of(active, block_id * model_width), out_back) for block_id in range(blocks)
    ]
    row_total = lax.psum_scatter(
        jnp.concatenate(pieces, axis=1), "wide", scatter_dimension=0, tiled=True
    )
    owner_terms = jnp.einsum(
        "nsu,ruc->nsrc",
        slot_pick,
        row_total.reshape(shard_rows, unit_count, model_width),
        precision=HIGHEST,
    )
    slot_grad = lax.psum_scatter(owner_terms, "narrow", scatter_dimension=0, tiled=True)
    own_pick = lax.dynamic_index_in_dim(slot_pick, lax.axis_index("narrow"), 0, keepdims=False)
    filled = (jnp.sum(own_pick, axis=1) > 0.5)[None, :, None, None]
    slot_rate = jnp.einsum("su,u->s", own_pick, unit_rates(), precision=HIGHEST)[
        None, :, None, None
    ]
    new_state = adam_update(masters, first_moment, second_moment, average, slot_grad, slot_rate)
    new_masters, new_first, new_second, new_average = [
        jnp.where(filled, state_part, 0.0) for state_part in new_state
    ]
    vec_new_value, vec_new_first, vec_new_second, vec_new_average = adam_update(
        vec_value, vec_first, vec_second, vec_average, vector_total, vector_rate
    )
    return (
        layer_out,
        patch_grad,
        text_grad,
        new_masters,
        new_first,
        new_second,
        new_average,
        new_masters.astype(jnp.bfloat16),
        vec_new_value,
        vec_new_first,
        vec_new_second,
        vec_new_average,
    )


def solution(mesh):
    in_specs = (
        P(("wide", "narrow"), None),
        P("narrow", None, "wide"),
        P(("wide", "narrow"), None),
        P(("wide", "narrow"), None),
        P(),
        P("narrow", None, "wide", None),
        P("narrow", None, "wide", None),
        P("narrow", None, "wide", None),
        P("narrow", None, "wide", None),
        P(),
        P(),
        P(),
        P(),
    )
    out_specs = (
        P(("wide", "narrow"), None),
        P(("wide", "narrow"), None),
        P("narrow", None, "wide"),
        P("narrow", None, "wide", None),
        P("narrow", None, "wide", None),
        P("narrow", None, "wide", None),
        P("narrow", None, "wide", None),
        P("narrow", None, "wide", None),
        P(),
        P(),
        P(),
        P(),
    )
    return jax.shard_map(local, mesh=mesh, in_specs=in_specs, out_specs=out_specs, check_vma=False)
```

profile of v0, /device:TPU:0, one launch (start us, length us, event | category | flops | bytes accessed | tf_op | source)
XLA Modules:
  0.0 822.0 jit_solution(1800503005500715682)
XLA Ops:
  9.1 53.7 %all-gather.3.cloned.1.call-done = bf16[1,4,512,512]{3,2,1,0:T(8,128)(2,1)} async-done(((bf16[1,4,64,512]{3,2,1,0:T(8,128)(2,1)}), bf16[1,4,512,512]{3,2,1,0:T(8,128)(2,1)}) %all-gather.3.cloned.1.call-update) | async-done | bytes 2097168 | tf_op jit(solution)/shard_map/all_gather | solution.py:117
  63.0 30.5 %all_gather.11 = bf16[1,77,512]{1,2,0:T(8,128)(2,1)S(1)} all-gather(bf16[1,77,64]{1,2,0:T(8,128)(2,1)S(1)} %copy-done.54), channel_id=1, replica_groups=mesh['wide'=8,'narrow'=4] {'wide'}, dimensions={2}, use_global_device_ids=true | all-gather | bytes 88704 | tf_op jit(solution)/shard_map/all_gather | solution.py:129
  101.7 19.5 %all-gather.5.cloned.1.call-done = bf16[4,4,512,512]{3,2,1,0:T(8,128)(2,1)} async-done(((bf16[1,4,512,512]{3,2,1,0:T(8,128)(2,1)}), bf16[4,4,512,512]{3,2,1,0:T(8,128)(2,1)}) %all-gather.5.cloned.1.call-update) | async-done | bytes 8388624 | tf_op jit(solution)/shard_map/all_gather | solution.py:118
  121.2 7.6 gather_fusion
  128.8 3.6 broadcast_select_fusion
  141.9 3.8 copy.134
  145.7 3.8 copy.132
  149.5 3.7 copy.131
  153.2 74.6 %while.30 = (s32[]{:T(128)}, bf16[8,1280,64]{1,2,0:T(8,128)(2,1)S(1)}, f32[8,1280]{1,0:T(8,128)S(1)}, pred[1280]{0:T(1024)(128)(4,1)S(1)}, bf16[8,1280,64]{2,1,0...) while((s32[]{:T(128)}, ...), condition=%wide.region_11.12_spmd, body=%wide.region_6.11_spmd.sunk | while | flops 458621440 | bytes 23153020 | solution.py:178
  176.8 3.0 fusion.244
  232.8 31.1 %multiply_convert_fusion.2 = (bf16[1280,2048]{1,0:T(8,128)(2,1)}, f32[1280,2048]{1,0:T(8,128)}, f32[1280,2048]{1,0:T(8,128)}) fusion(f32[2048]{0:T(1024)S(1)} %slice.66, bf16[512,512]{1,0:T(8,128)(2,1)S(1)} %copy-done.29, bf16[512,512]{1,0:T(8,128)(2,1)S(1)} %copy-done.30, bf16[512,512]{1,0:T(8,128)(2,1)S(1)} %copy-done.31, ...), kind=kOutput, calls=%fused_computation.108 | convolution fusion | flops 2869035008 | bytes 30955520 | tf_op jit(solution)/shard_map/dot_general | solution.py:25
  263.9 13.9 %convert_reduce_fusion = (f32[2048]{0:T(1024)}, bf16[1280,2048]{1,0:T(8,128)(2,1)S(1)}) fusion(f32[1280,2048]{1,0:T(8,128)} %get-tuple-element.328, bf16[512,512]{1,0:T(8,128)(2,1)S(1)} %copy-done.26, bf16[512,512]{1,0:T(8,128)(2,1)S(1)} %copy-done.27, bf16[512,512]{1,0:T(8,128)(2,1)S(1)} %copy-done.28, bf16[512,512]{1,0:T(8,128)(2,1)S(1)} %copy-done.24, ...), kind=kOutput, calls=%fused_computation.106 | convolution fusion | flops 2737960960 | bytes 29639936 | tf_op jit(solution)/shard_map/dot_general | solution.py:35
  277.9 5.0 fusion.174
  282.8 3.4 copy.139
  296.1 156.4 %while.31 = (s32[]{:T(128)}, bf16[8,1280,64]{1,2,0:T(8,128)(2,1)}, bf16[8,1280,64]{1,2,0:T(8,128)(2,1)}, bf16[8,1280,64]{1,2,0:T(8,128)(2,1)}, bf16[8,77,64]{1,2...) while((s32[]{:T(128)}, bf16[8,1280,64]{1,2,0:T(8,128)(2,1)}, ...), condition=%wide.region_19.20_spmd, body=%wide.region_16.19_spmd.sunk | while | flops 1127437824 | bytes 57579420 | solution.py:221
  300.1 3.0 fusion.263
  319.6 3.0 fusion.263
  339.1 3.0 fusion.263
  358.7 3.0 fusion.263
  378.2 3.0 fusion.263
  397.7 3.0 fusion.263
  417.3 3.0 fusion.263
  436.8 3.0 fusion.263
  461.4 3.6 convolution_dynamic-update-slice_fusion.6
  469.1 7.7 convolution_dynamic-update-slice_fusion
  476.8 3.4 convolution_dynamic-update-slice_fusion.4
  480.2 3.3 convolution_dynamic-update-slice_fusion.3
  490.1 7.0 fusion.100
  502.3 192.7 %reduce-scatter.6.cloned.1.call-done = f32[64,6144]{1,0:T(8,128)} async-done(((f32[512,6144]{1,0:T(8,128)}), f32[64,6144]{1,0:T(8,128)}) %reduce-scatter.6.cloned.1.call-update) | async-done | bytes 1572880 | tf_op jit(solution)/shard_map/reduce_scatter | solution.py:264
  714.4 39.7 %psum.7 = f32[4608]{0:T(1024)S(1)} all-reduce(f32[4608]{0:T(1024)S(1)} %constant_dynamic-update-slice_fusion.3), channel_id=1, replica_groups=mesh['wide'=8,'narrow'=4] {'wide','narrow'}, use_global_device_ids=true, to_apply=%region_36.37 | all-reduce | flops 4608 | bytes 36864 | tf_op jit(solution)/shard_map/psum | solution.py:246
  754.8 3.2 fusion.167
  759.0 56.3 %reduce-scatter.4.cloned.1.call-done = f32[1,77,64]{1,0,2:T(1,128)} async-done(((f32[1,77,512]{1,0,2:T(1,128)}), f32[1,77,64]{1,0,2:T(1,128)}) %reduce-scatter.4.cloned.1.call-update) | async-done | bytes 19728 | tf_op jit(solution)/shard_map/reduce_scatter | solution.py:247
  (431 shorter events, 282.3 us)
Async XLA Ops:
  7.2 55.8 %copy-start.43 = (f32[4608]{0:T(1024)S(1)}, f32[4608]{0:T(1024)}, u32[]{:S(2)}) copy-start(f32[4608]{0:T(1024)} %param.27) | copy-start | bytes 55300
  7.2 55.8 %copy-start.54 = (bf16[1,77,64]{1,2,0:T(8,128)(2,1)S(1)}, bf16[1,77,64]{1,2,0:T(8,128)(2,1)}, u32[]{:S(2)}) copy-start(bf16[1,77,64]{1,2,0:T(8,128)(2,1)} %param.19) | copy-start | bytes 29572
  7.2 55.6 %all-gather.3.cloned.1.call-start = ((), (), s32[]{:S(2)}) async-start(), calls=%async_computation.3 | async-start | bytes 2359296 | tf_op jit(solution)/shard_map/all_gather | solution.py:117
  9.0 112.1 %all-gather.5.cloned.1.call-start = ((), (), s32[]{:S(2)}) async-start(), calls=%async_computation.4 | async-start | bytes 10485760 | tf_op jit(solution)/shard_map/all_gather | solution.py:118
  62.8 632.2 %reduce-scatter.6.cloned.1.call-start = ((), (), s32[]{:S(2)}) async-start(), calls=%async_computation.6 | async-start | bytes 14155776 | tf_op jit(solution)/shard_map/reduce_scatter | solution.py:264
  93.6 39.0 %copy-start.13 = (bf16[1,77,512]{2,1,0:T(8,128)(2,1)}, bf16[1,77,512]{2,1,0:T(8,128)(2,1)S(1)}, u32[]{:S(2)}) copy-start(bf16[1,77,512]{2,1,0:T(8,128)(2,1)S(1)} %copy.133) | copy-start | bytes 236548
  95.3 132.6 %copy-start = (bf16[1280,512]{0,1:T(8,128)(2,1)}, bf16[1280,512]{0,1:T(8,128)(2,1)S(1)}, u32[]{:S(2)}) copy-start(bf16[1280,512]{0,1:T(8,128)(2,1)S(1)} %copy.130) | copy-start | bytes 3932164
  98.7 34.0 %copy-start.52 = (f32[77]{0:T(128)}, f32[77]{0:T(128)S(1)}, u32[]{:S(2)}) copy-start(f32[77]{0:T(128)S(1)} %broadcast_multiply_fusion.2) | copy-start | bytes 928
  99.1 29.7 %copy-start.37 = (f32[1280]{0:T(1024)}, f32[1280]{0:T(1024)S(1)}, u32[]{:S(2)}) copy-start(f32[1280]{0:T(1024)S(1)} %broadcast_multiply_fusion.1) | copy-start | bytes 15364
  99.5 29.3 %copy-start.45 = (f32[1280]{0:T(1024)}, f32[1280]{0:T(1024)S(1)}, u32[]{:S(2)}) copy-start(f32[1280]{0:T(1024)S(1)} %fusion.106) | copy-start | bytes 15364
  99.5 33.1 %copy-start.56 = (f32[77]{0:T(128)}, f32[77]{0:T(128)S(1)}, u32[]{:S(2)}) copy-start(f32[77]{0:T(128)S(1)} %fusion.149) | copy-start | bytes 928
  100.1 32.6 %copy-start.39 = (f32[512]{0:T(512)}, f32[512]{0:T(512)S(1)}, u32[]{:S(2)}) copy-start(f32[512]{0:T(512)S(1)} %get-tuple-element.355) | copy-start | bytes 6148
  100.1 32.6 %copy-start.47 = (f32[512]{0:T(512)}, f32[512]{0:T(512)S(1)}, u32[]{:S(2)}) copy-start(f32[512]{0:T(512)S(1)} %get-tuple-element.354) | copy-start | bytes 6148
  100.1 130.5 %copy-start.60 = (f32[512]{0:T(512)}, f32[512]{0:T(512)S(1)}, u32[]{:S(2)}) copy-start(f32[512]{0:T(512)S(1)} %get-tuple-element.352) | copy-start | bytes 6148
  100.1 28.7 %copy-start.41 = (f32[1280]{0:T(1024)}, f32[1280]{0:T(1024)S(1)}, u32[]{:S(2)}) copy-start(f32[1280]{0:T(1024)S(1)} %fusion.146) | copy-start | bytes 15364
  132.4 7.1 copy-start.5
  230.3 33.6 %copy-start.2 = (f32[1280,512]{0,1:T(8,128)}, f32[1280,512]{0,1:T(8,128)S(1)}, u32[]{:S(2)}) copy-start(f32[1280,512]{0,1:T(8,128)S(1)} %get-tuple-element.357) | copy-start | bytes 7864324
  232.7 31.1 %copy-start.9 = (bf16[1280,512]{0,1:T(8,128)(2,1)S(1)}, bf16[1280,512]{0,1:T(8,128)(2,1)}, u32[]{:S(2)}) copy-start(bf16[1280,512]{0,1:T(8,128)(2,1)} %copy.138) | copy-start | bytes 3932164
  232.7 31.1 %copy-start.24 = (bf16[512,512]{1,0:T(8,128)(2,1)S(1)}, bf16[512,512]{1,0:T(8,128)(2,1)}, u32[]{:S(2)}) copy-start(bf16[512,512]{1,0:T(8,128)(2,1)} %get-tuple-element.339) | copy-start | bytes 1572868
  232.7 31.2 %copy-start.26 = (bf16[512,512]{1,0:T(8,128)(2,1)S(1)}, bf16[512,512]{1,0:T(8,128)(2,1)}, u32[]{:S(2)}) copy-start(bf16[512,512]{1,0:T(8,128)(2,1)} %get-tuple-element.340) | copy-start | bytes 1572868
  232.7 31.2 %copy-start.27 = (bf16[512,512]{1,0:T(8,128)(2,1)S(1)}, bf16[512,512]{1,0:T(8,128)(2,1)}, u32[]{:S(2)}) copy-start(bf16[512,512]{1,0:T(8,128)(2,1)} %get-tuple-element.341) | copy-start | bytes 1572868
  232.8 31.2 %copy-start.28 = (bf16[512,512]{1,0:T(8,128)(2,1)S(1)}, bf16[512,512]{1,0:T(8,128)(2,1)}, u32[]{:S(2)}) copy-start(bf16[512,512]{1,0:T(8,128)(2,1)} %get-tuple-element.342) | copy-start | bytes 1572868
  469.1 7.7 copy-start.11
  487.5 267.4 %reduce-scatter.8.cloned.1.call-start = ((), (), s32[]{:S(2)}) async-start(), calls=%async_computation.7 | async-start | bytes 2621440 | tf_op jit(solution)/shard_map/reduce_scatter | solution.py:273
  700.5 114.8 %reduce-scatter.4.cloned.1.call-start = ((), (), s32[]{:S(2)}) async-start(), calls=%async_computation.5 | async-start | bytes 294912 | tf_op jit(solution)/shard_map/reduce_scatter | solution.py:247
  712.1 42.0 %copy-start.44 = (f32[4608]{0:T(1024)S(1)}, f32[4608]{0:T(1024)}, u32[]{:S(2)}) copy-start(f32[4608]{0:T(1024)} %param.27) | copy-start | bytes 55300
  712.1 42.0 %copy-start.49 = (f32[4608]{0:T(1024)S(1)}, f32[4608]{0:T(1024)}, u32[]{:S(2)}) copy-start(f32[4608]{0:T(1024)} %param.30) | copy-start | bytes 55300
  712.2 42.0 %copy-start.50 = (f32[4608]{0:T(1024)S(1)}, f32[4608]{0:T(1024)}, u32[]{:S(2)}) copy-start(f32[4608]{0:T(1024)} %param.28) | copy-start | bytes 55300
  712.2 42.0 %copy-start.51 = (f32[4608]{0:T(1024)S(1)}, f32[4608]{0:T(1024)}, u32[]{:S(2)}) copy-start(f32[4608]{0:T(1024)} %param.29) | copy-start | bytes 55300
  712.2 42.7 %copy-start.17 = (f32[1,4,64,512]{3,2,1,0:T(8,128)S(1)}, f32[1,4,64,512]{3,2,1,0:T(8,128)}, u32[]{:S(2)}) copy-start(f32[1,4,64,512]{3,2,1,0:T(8,128)} %param.23) | copy-start | bytes 1572868
  712.2 42.6 %copy-start.58 = (f32[4]{0:T(128)S(1)}, f32[4]{0:T(128)}, u32[]{:S(2)}) copy-start(f32[4]{0:T(128)} %convolution_bitcast_fusion.1) | copy-start | bytes 52
  714.3 43.7 %copy-start.35 = (f32[1,4,64,512]{3,2,1,0:T(8,128)S(1)}, f32[1,4,64,512]{3,2,1,0:T(8,128)}, u32[]{:S(2)}) copy-start(f32[1,4,64,512]{3,2,1,0:T(8,128)} %param.26) | copy-start | bytes 1572868
  (45 other events, 114.9 us)
Sparse Core Ops, SparseCore 0:
  10.8 51.9 all-gather.2
  64.3 56.7 all-gather.4
  487.6 207.3 reduce-scatter.5
  700.6 31.1 reduce-scatter.7
  754.3 60.9 reduce-scatter.3
where the time goes:
time: 835 us; the launch traced here: 822 us
  matrix products  323 us (39%)
  waiting for transfers between devices  322 us (39%)
  blocking collectives  70.3 us (8%)
  local copies, waits for them, and re-layouts  52.1 us (6%)
  other arithmetic  37.8 us (5%)
  between operations  15 us (2%)
    reduce_scatter x1, waiting for transfers between devices, local(): lax.psum_scatter(jnp.concatenate(pieces, axis=1), 'wide', scatter_dimensi...  193 us
    dot_general x56, matrix products, rmatmul(): lax.dot_general(left_side, right_side, (((1,), (1,)), ((), ())), preferre...  122 us
    dot_general x40, matrix products, matmul(): return jnp.dot(left_side, right_side, preferred_element_type=jnp.float32)  102 us
    dot_general x43, matrix products, tmatmul(): lax.dot_general(left_side, right_side, (((0,), (0,)), ((), ())), preferre...  95.6 us
    reduce_scatter x1, waiting for transfers between devices, local(): lax.psum_scatter(text_back[None], 'wide', scatter_dimension=2, tiled=True)  56.3 us
    all_gather x1, waiting for transfers between devices, local(): row_full = lax.all_gather(own_copy, 'wide', axis=2, tiled=True)  53.7 us
    psum x1, blocking collectives, local(): vector_total = lax.psum(vector_grad, ('wide', 'narrow'))  39.7 us
    all_gather x1, blocking collectives, local(): lax.all_gather(text_tokens, 'wide', axis=2, tiled=True)[0]  30.5 us
  transfers between devices with their start and end apart: 5, of which 4 were waited for; matrix products, arithmetic and copies ran while one was open for 5% of the time, Pallas kernels for 0%

commit v1 on v0

v1 whole, which is shorter than its diff:
```python
import functools

import jax
import jax.numpy as jnp
from jax import lax
from jax.experimental import pallas as pl
from jax.experimental.pallas import tpu as pltpu
from jax.sharding import PartitionSpec as P

D = 512
HEADS = 8
FF = 2048
VIEWS = 5
VIEW_ROWS = 256
ROWS = VIEWS * VIEW_ROWS
LANG = 77
TEXT = 128
KEYS = ROWS + TEXT
STEP = 5
UNITS = 12
SLOTS = 4
VEC = 5 * D + FF
F32 = jnp.float32
BF16 = jnp.bfloat16
MESH = pl.DeviceIdType.MESH
NEG = -1e30

norm_eps = 1e-05
beta_one = 0.5
beta_two = 0.5
adam_eps = 1e-08
weight_decay = 0.1
average_keep = 0.75
vector_rate = 0.25
VMEM_LIMIT = 60 * 2**20


def dot(left, right, left_dim=1, right_dim=0):
    return lax.dot_general(
        left, right, (((left_dim,), (right_dim,)), ((), ())), preferred_element_type=F32
    )


def vmem():
    return pl.BlockSpec(memory_space=pltpu.VMEM)


def smem():
    return pl.BlockSpec(memory_space=pltpu.SMEM)


def unit_ranks(owners_ref):
    owner = [owners_ref[u] for u in range(UNITS)]
    rank = []
    for u in range(UNITS):
        total = jnp.int32(0)
        for v in range(u):
            total = total + (owner[v] == owner[u]).astype(jnp.int32)
        rank.append(jnp.minimum(total, SLOTS - 1))
    return owner, rank


def normalize(values):
    center = values - jnp.mean(values, axis=-1, keepdims=True)
    spread = jnp.mean(center * center, axis=-1, keepdims=True)
    scale = lax.rsqrt(spread + norm_eps)
    return center * scale, scale


def norm_back(grads, gain, normed, scale):
    e = grads * gain
    return scale * (
        e
        - jnp.mean(e, axis=-1, keepdims=True)
        - normed * jnp.mean(e * normed, axis=-1, keepdims=True)
    )


def place():
    w = lax.axis_index("wide")
    n = lax.axis_index("narrow")
    return w, n, w // 2, w % 2, n // 2, n % 2


def greet(peers):
    barrier = pltpu.get_barrier_semaphore()
    for peer in peers:
        pl.semaphore_signal(barrier, inc=1, device_id=peer, device_id_type=MESH)
    pl.semaphore_wait(barrier, len(peers))


def all_peers(w, n, z, x):
    peers = [(w, lax.rem(n + k, 4)) for k in range(1, 4)]
    peers += [(lax.rem(z + k, 4) * 2 + x, n) for k in range(1, 4)]
    peers.append((z * 2 + 1 - x, n))
    return peers


class Sender:
    def __init__(self, send, recv):
        self.send, self.recv, self.count = send, recv, 0

    def __call__(self, src, dst, device):
        i = self.count
        self.count += 1
        copy = pltpu.make_async_remote_copy(
            src_ref=src,
            dst_ref=dst,
            send_sem=self.send.at[i],
            recv_sem=self.recv.at[i],
            device_id=device,
            device_id_type=MESH,
        )
        copy.start()
        return copy


def pipeline(groups, stages):
    flying = {}
    for step in range(groups + len(stages)):
        for s in reversed(range(len(stages) + 1)):
            g = step - s
            if not 0 <= g < groups:
                continue
            if s > 0:
                copies, after = flying.pop((g, s - 1))
                for copy in copies:
                    copy.wait()
                if after is not None:
                    after()
            if s < len(stages):
                flying[(g, s)] = stages[s](g)


def gather_kernel(owners, masters, text, w_out, t_out, send_buf, slot_buf, text_buf, send, recv):
    w, n, z, x, y, c = place()
    for q in range(4):
        send_buf[q] = masters[0, :, :, q * 128 : (q + 1) * 128].astype(BF16)
    text_buf[...] = jnp.zeros_like(text_buf)
    text_buf[0:LANG, 0:64] = text[0].astype(F32)
    t_out[z, x] = text_buf[...].T[0:64].astype(BF16)
    greet(all_peers(w, n, z, x))
    go = Sender(send, recv)
    first = []
    for k in range(1, 4):
        q = lax.rem(n + k, 4)
        first.append(go(send_buf.at[q], slot_buf.at[n], (w, q)))
    text_copies = [
        go(t_out.at[z, x], t_out.at[z, x], (lax.rem(z + k, 4) * 2 + x, n)) for k in range(1, 4)
    ]
    slot_buf[n] = send_buf[n]
    owner, rank = unit_ranks(owners)
    for copy in first:
        copy.wait()
    quarter = pl.ds(pl.multiple_of(n * 128, 128), 128)
    for u in range(UNITS):
        w_out[u, z, x, :, quarter] = slot_buf[owner[u], rank[u]]
    for copy in text_copies:
        copy.wait()
    text_last = go(t_out.at[:, x], t_out.at[:, x], (z * 2 + 1 - x, n))

    def cols(q):
        return pl.ds(pl.multiple_of(q * 128, 128), 128)

    def share(ref, device):
        return go(ref, ref, device)

    to_x = (z * 2 + 1 - x, n)
    to_y = (w, (1 - y) * 2 + c)
    to_c = (w, y * 2 + 1 - c)

    def stage_z(g):
        piece = w_out.at[pl.ds(3 * g, 3), z, x, :, cols(n)]
        return [share(piece, (lax.rem(z + k, 4) * 2 + x, n)) for k in range(1, 4)], None

    def stage_one(g):
        u = pl.ds(3 * g, 3)
        return [
            share(w_out.at[u, pl.ds(0, 2), x, :, cols(n)], to_x),
            share(w_out.at[u, pl.ds(2, 2), x, :, cols(n)], to_y),
        ], None

    def stage_two(g):
        u = pl.ds(3 * g, 3)
        return [
            share(w_out.at[u, pl.ds(0, 2), :, :, cols(n)], to_y),
            share(w_out.at[u, pl.ds(2, 2), x, :, cols(c)], to_x),
            share(w_out.at[u, pl.ds(2, 2), x, :, cols(2 + c)], to_x),
        ], None

    def stage_core(g):
        u = pl.ds(3 * g, 3)
        return [
            share(w_out.at[u, :, :, :, cols(c)], to_c),
            share(w_out.at[u, :, :, :, cols(2 + c)], to_c),
        ], None

    pipeline(4, [stage_z, stage_one, stage_two, stage_core])
    text_last.wait()


def gather(owners, masters, text):
    if lax.axis_size("wide") != 8 or lax.axis_size("narrow") != 4:
        packed = lax.all_gather(masters.astype(BF16), "wide", axis=2, tiled=True)
        packed = lax.all_gather(packed, "narrow", axis=0, tiled=True)
        same = owners[:, None] == owners[None, :]
        ids = jnp.arange(UNITS)
        rank = jnp.sum((same & (ids[None, :] < ids[:, None])).astype(jnp.int32), axis=1)
        units = jnp.take(packed.reshape(-1, D, D), owners * SLOTS + rank, axis=0)
        rows = lax.all_gather(text, "wide", axis=2, tiled=True)[0]
        return units, jnp.pad(rows.T, ((0, 0), (0, TEXT - LANG)))
    copies = 3 + 3 + 1 + 4 * 10
    units, text_t = pl.pallas_call(
        gather_kernel,
        out_shape=[
            jax.ShapeDtypeStruct((UNITS, 4, 2, 64, D), BF16),
            jax.ShapeDtypeStruct((4, 2, 64, TEXT), BF16),
        ],
        in_specs=[smem(), vmem(), vmem()],
        out_specs=[vmem(), vmem()],
        scratch_shapes=[
            pltpu.VMEM((4, SLOTS, 64, 128), BF16),
            pltpu.VMEM((4, SLOTS, 64, 128), BF16),
            pltpu.VMEM((128, 128), F32),
            pltpu.SemaphoreType.DMA((copies,)),
            pltpu.SemaphoreType.DMA((copies,)),
        ],
        compiler_params=pltpu.CompilerParams(
            collective_id=1, has_side_effects=True, vmem_limit_bytes=VMEM_LIMIT
        ),
    )(owners, masters, text)
    return units.reshape(UNITS, D, D), text_t.reshape(D, TEXT)


def live_column(counts, rows):
    index = lax.broadcasted_iota(jnp.int32, (VIEW_ROWS, 1), 0)
    return [(index < counts[0, v]) for v in range(rows // VIEW_ROWS)]


def forward_kernel(
    counts, x, text_t, vec, w, att_t, probs, inverse, q_t, keyed, v_t, normed, text_normed
):
    i = pl.program_id(0)

    @pl.when(i == 0)
    def _():
        gain, bias = vec[:, 0:D], vec[:, D : 2 * D]
        normed[...] = (normalize(x[...].astype(F32))[0] * gain + bias).astype(BF16)
        rows = text_t[...].astype(F32).T
        live_text = lax.broadcasted_iota(jnp.int32, (TEXT, 1), 0) < LANG
        text_normed[...] = jnp.where(
            live_text, normalize(rows)[0] * gain + bias, 0.0
        ).astype(BF16)
        q_t[...] = dot(w[0], normed[...], 0, 1).astype(BF16) * BF16(0.125)
        v_t[:, 0:ROWS] = dot(w[2], normed[...], 0, 1).astype(BF16)
        v_t[:, ROWS:KEYS] = dot(w[2], text_normed[...], 0, 1).astype(BF16)
        for p in range(4):
            pair = slice(p * 128, (p + 1) * 128)
            keyed[p, 0:ROWS, 0:128] = dot(normed[...], w[1, :, pair]).astype(BF16)
            keyed[p, ROWS:KEYS, 0:128] = dot(text_normed[...], w[1, :, pair]).astype(BF16)
            for v, live in enumerate(live_column(counts, ROWS)):
                keyed[p, v * VIEW_ROWS : (v + 1) * VIEW_ROWS, 128:256] = jnp.broadcast_to(
                    jnp.where(live, 0.0, NEG), (VIEW_ROWS, 128)
                ).astype(BF16)
            keyed[p, ROWS:KEYS, 128:256] = jnp.broadcast_to(
                jnp.where(live_text, 0.0, NEG), (TEXT, 128)
            ).astype(BF16)

    row = lax.broadcasted_iota(jnp.int32, (128, ROWS), 0)
    one = jnp.where(row == 0, 1.0, 0.0).astype(BF16)
    pair_q = q_t[pl.ds(pl.multiple_of(i * 128, 128), 128), :]
    for h in range(2):
        mine = (row >= 64 * h) & (row < 64 * h + 64)
        q = jnp.where(mine, pair_q, jnp.zeros_like(pair_q))
        scores = dot(keyed[i], jnp.concatenate([q, one], axis=0))
        peak = jnp.max(scores, axis=0, keepdims=True)
        e = jnp.exp(scores - peak)
        total = jnp.sum(e, axis=0, keepdims=True)
        low = e.astype(BF16)
        probs[h] = low
        mixed = dot(v_t[pl.ds(pl.multiple_of(i * 128 + h * 64, 64), 64), :], low)
        inv = 1.0 / total
        att_t[h * 64 : (h + 1) * 64, :] = (mixed * inv).astype(BF16)
        inverse[0, h : h + 1, :] = inv


def attention_forward(counts, x, text_t, vec, units):
    return pl.pallas_call(
        forward_kernel,
        grid=(4,),
        in_specs=[smem(), vmem(), vmem(), vmem(), pl.BlockSpec((3, D, D), lambda i: (0, 0, 0))],
        out_specs=[
            pl.BlockSpec((128, ROWS), lambda i: (i, 0)),
            pl.BlockSpec((2, KEYS, ROWS), lambda i: (i, 0, 0)),
            pl.BlockSpec((1, 2, ROWS), lambda i: (i, 0, 0)),
            pl.BlockSpec((D, ROWS), lambda i: (0, 0)),
            pl.BlockSpec((4, KEYS, 256), lambda i: (0, 0, 0)),
            pl.BlockSpec((D, KEYS), lambda i: (0, 0)),
        ],
        out_shape=[
            jax.ShapeDtypeStruct((D, ROWS), BF16),
            jax.ShapeDtypeStruct((HEADS, KEYS, ROWS), BF16),
            jax.ShapeDtypeStruct((4, 2, ROWS), F32),
            jax.ShapeDtypeStruct((D, ROWS), BF16),
            jax.ShapeDtypeStruct((4, KEYS, 256), BF16),
            jax.ShapeDtypeStruct((D, KEYS), BF16),
        ],
        scratch_shapes=[pltpu.VMEM((ROWS, D), BF16), pltpu.VMEM((TEXT, D), BF16)],
        compiler_params=pltpu.CompilerParams(vmem_limit_bytes=VMEM_LIMIT),
    )(counts, x, text_t, vec, units)


def dense_kernel(
    counts, att_t, x, g, vec, w,
    layer_out, middle_back, back_t, grads, gain_grad, bias_grad, up_grad, down_grad,
    total, *, tile
):
    i = pl.program_id(0)
    steps = pl.num_programs(0)
    gain, bias = vec[:, 2 * D : 3 * D], vec[:, 3 * D : 4 * D]
    a = att_t[...]
    index = lax.broadcasted_iota(jnp.int32, (tile, 1), 0) + i * tile
    live = jnp.zeros((tile, 1), jnp.bool_)
    for v in range(VIEWS):
        live = live | ((index >= v * VIEW_ROWS) & (index < v * VIEW_ROWS + counts[0, v]))
    middle = x[...].astype(F32) + dot(a, w[3], 0, 0)
    normed, scale = normalize(middle)
    low = (normed * gain + bias).astype(BF16)
    out_back = jnp.where(live, g[...].astype(F32), 0.0)
    out_low = out_back.astype(BF16)

    @pl.when(i == 0)
    def _():
        total[...] = jnp.zeros_like(total)
        gain_grad[...] = jnp.zeros_like(gain_grad)
        bias_grad[...] = jnp.zeros_like(bias_grad)
        up_grad[...] = jnp.zeros_like(up_grad)
        down_grad[...] = jnp.zeros_like(down_grad)

    out = middle + vec[:, 4 * D + FF :]
    normed_back = jnp.zeros((tile, D), F32)
    for j in range(4):
        block = slice(j * D, (j + 1) * D)
        preact = dot(low, w[4 + j]) + vec[:, 4 * D + j * D : 5 * D + j * D]
        phi = 0.5 + 0.5 * lax.erf(preact * 0.7071067811865476)
        active = (preact * phi).astype(BF16)
        slope = phi + preact * (jnp.exp(-0.5 * preact * preact) * 0.3989422804014327)
        out = out + dot(active, w[8 + j])
        preact_back = (dot(out_low, w[8 + j], 1, 1) * slope).astype(BF16)
        normed_back = normed_back + dot(preact_back, w[4 + j], 1, 1)
        total[1 + j] += dot(low, preact_back, 0, 0)
        total[5 + j] += dot(active, out_low, 0, 0)
        up_grad[:, block] += jnp.sum(preact_back.astype(F32), axis=0, keepdims=True)
    layer_out[...] = jnp.where(live, out, 0.0).astype(BF16)
    back = out_back + norm_back(normed_back, gain, normed, scale)
    middle_back[...] = back
    branch = back.astype(BF16)
    back_t[...] = dot(w[3], branch, 1, 1).astype(BF16)
    total[0] += dot(a, branch)
    gain_grad[...] += jnp.sum(normed_back * normed, axis=0, keepdims=True)
    bias_grad[...] += jnp.sum(normed_back, axis=0, keepdims=True)
    down_grad[...] += jnp.sum(out_back, axis=0, keepdims=True)

    @pl.when(i == steps - 1)
    def _():
        grads[...] = total[...].astype(BF16)


def dense(counts, att_t, x, g, vec, units, tile=640):
    rows = pl.BlockSpec((tile, D), lambda i: (i, 0))
    columns = pl.BlockSpec((D, tile), lambda i: (0, i))
    return pl.pallas_call(
        functools.partial(dense_kernel, tile=tile),
        grid=(ROWS // tile,),
        in_specs=[smem(), columns, rows, rows, vmem(), vmem()],
        out_specs=[
            rows,
            rows,
            columns,
            pl.BlockSpec((9, D, D), lambda i: (0, 0, 0)),
            pl.BlockSpec((1, D), lambda i: (0, 0)),
            pl.BlockSpec((1, D), lambda i: (0, 0)),
            pl.BlockSpec((1, FF), lambda i: (0, 0)),
            pl.BlockSpec((1, D), lambda i: (0, 0)),
        ],
        out_shape=[
            jax.ShapeDtypeStruct((ROWS, D), BF16),
            jax.ShapeDtypeStruct((ROWS, D), F32),
            jax.ShapeDtypeStruct((D, ROWS), BF16),
            jax.ShapeDtypeStruct((9, D, D), BF16),
            jax.ShapeDtypeStruct((1, D), F32),
            jax.ShapeDtypeStruct((1, D), F32),
            jax.ShapeDtypeStruct((1, FF), F32),
            jax.ShapeDtypeStruct((1, D), F32),
        ],
        scratch_shapes=[pltpu.VMEM((9, D, D), F32)],
        compiler_params=pltpu.CompilerParams(vmem_limit_bytes=VMEM_LIMIT),
    )(counts, att_t, x, g, vec, units)


def backward_kernel(probs, inverse, keyed, v_t, back_t, q_t, att_t, query_back, key_back, value_back):
    row = lax.broadcasted_iota(jnp.int32, (128, ROWS), 0)
    lane = lax.broadcasted_iota(jnp.int32, (KEYS, 128), 1)
    ones = jnp.where(lane < 2, 1.0, 0.0).astype(BF16)
    value = jnp.concatenate([v_t[...].astype(F32).T.astype(BF16), ones], axis=1)
    key_t = keyed[:, 0:128].astype(F32).T.astype(BF16)
    back = back_t[...].astype(F32)
    product = back * att_t[...].astype(F32)
    query = q_t[...].astype(F32)
    key_total = jnp.zeros((KEYS, 128), F32)
    value_total = jnp.zeros((KEYS, 128), F32)
    for h in range(2):
        half = slice(h * 64, (h + 1) * 64)
        inv = inverse[0, h : h + 1, :]
        delta = jnp.sum(product[half], axis=0, keepdims=True) * inv
        high = delta.astype(BF16).astype(F32)
        mine = (row >= 64 * h) & (row < 64 * h + 64)
        scaled = jnp.where(mine, back * inv, 0.0)
        tail = jnp.where(row == 0, -high, jnp.where(row == 1, high - delta, 0.0))
        right = jnp.concatenate([scaled.astype(BF16), tail.astype(BF16)], axis=0)
        low = probs[h]
        score_back = low * dot(value, right).astype(BF16)
        query_back[half, :] = (dot(key_t[half], score_back) * 0.125).astype(BF16)
        key_total += dot(score_back, jnp.where(mine, query, 0.0).T.astype(BF16))
        value_total += dot(low, scaled.T.astype(BF16))
    key_back[...] = key_total.astype(BF16)
    value_back[...] = value_total.astype(BF16)


def attention_backward(probs, inverse, keyed, v_t, back_t, q_t, att_t):
    return pl.pallas_call(
        backward_kernel,
        grid=(4,),
        in_specs=[
            pl.BlockSpec((2, KEYS, ROWS), lambda i: (i, 0, 0)),
            pl.BlockSpec((1, 2, ROWS), lambda i: (i, 0, 0)),
            pl.BlockSpec((None, KEYS, 256), lambda i: (i, 0, 0)),
            pl.BlockSpec((128, KEYS), lambda i: (i, 0)),
            pl.BlockSpec((128, ROWS), lambda i: (i, 0)),
            pl.BlockSpec((128, ROWS), lambda i: (i, 0)),
            pl.BlockSpec((128, ROWS), lambda i: (i, 0)),
        ],
        out_specs=[
            pl.BlockSpec((128, ROWS), lambda i: (i, 0)),
            pl.BlockSpec((KEYS, 128), lambda i: (0, i)),
            pl.BlockSpec((KEYS, 128), lambda i: (0, i)),
        ],
        out_shape=[
            jax.ShapeDtypeStruct((D, ROWS), BF16),
            jax.ShapeDtypeStruct((KEYS, D), BF16),
            jax.ShapeDtypeStruct((KEYS, D), BF16),
        ],
        compiler_params=pltpu.CompilerParams(vmem_limit_bytes=VMEM_LIMIT),
    )(probs, inverse, keyed, v_t, back_t, q_t, att_t)


def project_kernel(
    x, text_t, vec, w, middle_back, query_back, key_back, value_back, text_key, text_value,
    patch_grad, grads, gain_grad, bias_grad, text_grad_t, total
):
    i = pl.program_id(0)
    steps = pl.num_programs(0)
    gain, bias = vec[:, 0:D], vec[:, D : 2 * D]

    @pl.when(i == 0)
    def _():
        live = lax.broadcasted_iota(jnp.int32, (TEXT, 1), 0) < LANG
        normed, scale = normalize(text_t[...].astype(F32).T)
        low_t = jnp.where(live, normed * gain + bias, 0.0).T.astype(BF16)
        k, v = text_key[...], text_value[...]
        back = dot(k, w[1], 1, 1) + dot(v, w[2], 1, 1)
        text_grad_t[...] = norm_back(back, gain, normed, scale).T.astype(BF16)
        gain_grad[...] = jnp.sum(back * normed, axis=0, keepdims=True)
        bias_grad[...] = jnp.sum(back, axis=0, keepdims=True)
        total[0] = jnp.zeros((D, D), F32)
        total[1] = dot(low_t, k)
        total[2] = dot(low_t, v)

    normed, scale = normalize(x[...].astype(F32))
    low_t = (normed * gain + bias).T.astype(BF16)
    q, k, v = query_back[...], key_back[...], value_back[...]
    back = dot(q, w[0], 0, 1) + dot(k, w[1], 1, 1) + dot(v, w[2], 1, 1)
    patch_grad[...] = middle_back[...] + norm_back(back, gain, normed, scale)
    total[0] += dot(low_t, q, 1, 1)
    total[1] += dot(low_t, k)
    total[2] += dot(low_t, v)
    gain_grad[...] += jnp.sum(back * normed, axis=0, keepdims=True)
    bias_grad[...] += jnp.sum(back, axis=0, keepdims=True)

    @pl.when(i == steps - 1)
    def _():
        grads[...] = total[...].astype(BF16)


def project_back(x, text_t, vec, units, middle_back, query_back, key_back, value_back, tile=640):
    rows = pl.BlockSpec((tile, D), lambda i: (i, 0))
    text_rows = pl.BlockSpec((TEXT, D), lambda i: (ROWS // TEXT, 0))
    return pl.pallas_call(
        project_kernel,
        grid=(ROWS // tile,),
        in_specs=[
            rows,
            vmem(),
            vmem(),
            pl.BlockSpec((3, D, D), lambda i: (0, 0, 0)),
            rows,
            pl.BlockSpec((D, tile), lambda i: (0, i)),
            rows,
            rows,
            text_rows,
            text_rows,
        ],
        out_specs=[
            rows,
            pl.BlockSpec((3, D, D), lambda i: (0, 0, 0)),
            pl.BlockSpec((1, D), lambda i: (0, 0)),
            pl.BlockSpec((1, D), lambda i: (0, 0)),
            pl.BlockSpec((D, TEXT), lambda i: (0, 0)),
        ],
        out_shape=[
            jax.ShapeDtypeStruct((ROWS, D), F32),
            jax.ShapeDtypeStruct((3, D, D), BF16),
            jax.ShapeDtypeStruct((1, D), F32),
            jax.ShapeDtypeStruct((1, D), F32),
            jax.ShapeDtypeStruct((D, TEXT), BF16),
        ],
        scratch_shapes=[pltpu.VMEM((3, D, D), F32)],
        compiler_params=pltpu.CompilerParams(vmem_limit_bytes=VMEM_LIMIT),
    )(
        x, text_t, vec, units, middle_back, query_back, key_back, value_back, key_back, value_back
    )


def add(a, b):
    return (a.astype(F32) + b.astype(F32)).astype(BF16)


def reduce_kernel(
    owners, rest, first, text, gain_one, bias_one, gain_two, bias_two, up, down,
    slot_grad, text_out, vec_out,
    c_buf, c_sum, ya_buf, ya_sum, xb_buf, xb_sum, xa_buf, yb_buf, z_sum, z_buf, red, s_buf, r_buf,
    tx_buf, t_sum, tz_buf, v_own, v_buf, vz_buf, send, recv
):
    w, n, z, x, y, c = place()
    offset = 0
    for piece in (gain_one, bias_one, gain_two, bias_two, up, down):
        size = piece.shape[1]
        v_own[:, offset : offset + size] = piece[...]
        offset += size
    greet(all_peers(w, n, z, x))
    go = Sender(send, recv)
    to_x = (z * 2 + 1 - x, n)
    to_y = (w, (1 - y) * 2 + c)
    to_c = (w, y * 2 + 1 - c)

    def to_z(k):
        return (lax.rem(z + k, 4) * 2 + x, n)

    def cols(q):
        return pl.ds(pl.multiple_of(q * 128, 128), 128)

    def source(g):
        return (first, 0) if g == 3 else (rest, 3 * g)

    def units_of(g):
        return pl.ds(0, 3) if g == 3 else pl.ds(3 * (g + 1), 3)

    def vector_stage(s, device):
        if s == 0:
            sent = v_own
        else:
            sent = v_buf.at[s + 2]
        return go(sent, v_buf.at[s], device)

    vc = vector_stage(0, to_c)
    tx = go(text.at[:, 1 - x], tx_buf, to_x)

    def stage_core(g):
        ref, base = source(g)
        u, at = units_of(g), pl.ds(base, 3)
        copies = [
            go(ref.at[at, :, :, :, cols(2 * k + 1 - c)], c_buf.at[k, u], to_c) for k in range(2)
        ]

        def after():
            for k in range(2):
                c_sum[k, u] = add(ref[at, :, :, :, cols(2 * k + c)], c_buf[k, u])

        return copies, after

    def stage_one(g):
        u = units_of(g)
        copies = [
            go(c_sum.at[1 - y, u, pl.ds(0, 2)], ya_buf.at[u], to_y),
            go(c_sum.at[0, u, pl.ds(2, 2), 1 - x], xb_buf.at[0, u], to_x),
            go(c_sum.at[1, u, pl.ds(2, 2), 1 - x], xb_buf.at[1, u], to_x),
        ]

        def after():
            ya_sum[u] = add(c_sum[y, u, 0:2], ya_buf[u])
            for k in range(2):
                xb_sum[k, u] = add(c_sum[k, u, 2:4, x], xb_buf[k, u])

        return copies, after

    def stage_two(g):
        u = units_of(g)
        copies = [
            go(ya_sum.at[u, :, 1 - x], xa_buf.at[u], to_x),
            go(xb_sum.at[1 - y, u], yb_buf.at[u], to_y),
        ]

        def after():
            z_sum[u, 0:2] = add(ya_sum[u, :, x], xa_buf[u])
            z_sum[u, 2:4] = add(xb_sum[y, u], yb_buf[u])

        return copies, after

    def stage_z(g):
        u = units_of(g)
        copies = [
            go(z_sum.at[u, lax.rem(z + k, 4)], z_buf.at[k - 1, u], to_z(k)) for k in range(1, 4)
        ]

        def after():
            total = z_sum[u, z].astype(F32)
            for k in range(3):
                total = total + z_buf[k, u].astype(F32)
            red[u] = total.astype(BF16)

        return copies, after

    pipeline(4, [stage_core, stage_one, stage_two, stage_z])

    owner, rank = unit_ranks(owners)
    for q in range(4):
        for s in range(SLOTS):
            unit = jnp.int32(0)
            for u in range(UNITS):
                unit = unit + jnp.where((owner[u] == q) & (rank[u] == s), u, 0)
            s_buf[q, s] = red[jnp.minimum(unit, UNITS - 1)]
    last = []
    for k in range(1, 4):
        q = lax.rem(n + k, 4)
        last.append(go(s_buf.at[q], r_buf.at[n], (w, q)))
    r_buf[n] = s_buf[n]

    vc.wait()
    v_buf[3] = v_own[...] + v_buf[0]
    vy = vector_stage(1, to_y)
    tx.wait()
    t_sum[...] = add(text[:, x], tx_buf[...])
    tz = [go(t_sum.at[lax.rem(z + k, 4)], tz_buf.at[k - 1], to_z(k)) for k in range(1, 4)]
    vy.wait()
    v_buf[4] = v_buf[3] + v_buf[1]
    vx = vector_stage(2, to_x)
    vx.wait()
    vz_buf[z] = v_buf[4] + v_buf[2]
    vz = [go(vz_buf.at[z], vz_buf.at[z], to_z(k)) for k in range(1, 4)]
    for copy in tz:
        copy.wait()
    total = t_sum[z].astype(F32)
    for k in range(3):
        total = total + tz_buf[k].astype(F32)
    text_out[...] = total
    for copy in last:
        copy.wait()
    for q in range(4):
        for s in range(SLOTS):
            slot_grad[s, :, q * 128 : (q + 1) * 128] = r_buf[q, s].astype(F32)
    for copy in vz:
        copy.wait()
    vec_out[...] = (vz_buf[0] + vz_buf[1]) + (vz_buf[2] + vz_buf[3])


def reduce_all(owners, rest, first, text, vecs):
    wide = lax.axis_size("wide")
    if wide != 8 or lax.axis_size("narrow") != 4:
        vec = lax.psum(jnp.concatenate(vecs, axis=1), ("wide", "narrow"))
        text_sum = lax.psum_scatter(text.astype(F32), "wide", scatter_dimension=0, tiled=True)
        all_units = jnp.concatenate([first, rest], axis=0).astype(F32)
        rows = lax.psum_scatter(all_units, "wide", scatter_dimension=1, tiled=True)
        same = owners[:, None] == owners[None, :]
        ids = jnp.arange(UNITS)
        rank = jnp.sum((same & (ids[None, :] < ids[:, None])).astype(jnp.int32), axis=1)
        pick = (owners[None, None, :] == jnp.arange(lax.axis_size("narrow"))[:, None, None]) & (
            rank[None, None, :] == jnp.arange(SLOTS)[None, :, None]
        )
        terms = jnp.einsum("nsu,urc->nsrc", pick.astype(F32), rows, precision=lax.Precision.HIGHEST)
        slots = lax.psum_scatter(terms, "narrow", scatter_dimension=0, tiled=True)
        return slots[0], text_sum, vec
    copies = 1 + 1 + 4 * 10 + 3 + 1 + 3 + 1 + 3
    bf = lambda *s: pltpu.VMEM(s, BF16)
    return pl.pallas_call(
        reduce_kernel,
        out_shape=[
            jax.ShapeDtypeStruct((SLOTS, 64, D), F32),
            jax.ShapeDtypeStruct((64, TEXT), F32),
            jax.ShapeDtypeStruct((1, VEC), F32),
        ],
        in_specs=[smem()] + [vmem()] * 9,
        out_specs=[vmem()] * 3,
        scratch_shapes=[
            bf(2, UNITS, 4, 2, 64, 128),
            bf(2, UNITS, 4, 2, 64, 128),
            bf(UNITS, 2, 2, 64, 128),
            bf(UNITS, 2, 2, 64, 128),
            bf(2, UNITS, 2, 64, 128),
            bf(2, UNITS, 2, 64, 128),
            bf(UNITS, 2, 64, 128),
            bf(UNITS, 2, 64, 128),
            bf(UNITS, 4, 64, 128),
            bf(3, UNITS, 64, 128),
            bf(UNITS, 64, 128),
            bf(4, SLOTS, 64, 128),
            bf(4, SLOTS, 64, 128),
            bf(4, 64, TEXT),
            bf(4, 64, TEXT),
            bf(3, 64, TEXT),
            pltpu.VMEM((1, VEC), F32),
            pltpu.VMEM((5, 1, VEC), F32),
            pltpu.VMEM((4, 1, VEC), F32),
            pltpu.SemaphoreType.DMA((copies,)),
            pltpu.SemaphoreType.DMA((copies,)),
        ],
        compiler_params=pltpu.CompilerParams(
            collective_id=2, has_side_effects=True, vmem_limit_bytes=VMEM_LIMIT
        ),
    )(
        owners,
        rest.reshape(9, 4, 2, 64, D),
        first.reshape(3, 4, 2, 64, D),
        text.reshape(4, 2, 64, TEXT),
        *vecs,
    )


def adam(master, moment_one, moment_two, averaged, gradient, rate):
    moment_one = beta_one * moment_one + (1.0 - beta_one) * gradient
    moment_two = beta_two * moment_two + (1.0 - beta_two) * gradient * gradient
    mean_hat = moment_one / (1.0 - beta_one**STEP)
    second_hat = moment_two / (1.0 - beta_two**STEP)
    master = master - rate * (
        mean_hat / (jnp.sqrt(second_hat) + adam_eps) + weight_decay * master
    )
    averaged = average_keep * averaged + (1.0 - average_keep) * master
    return master, moment_one, moment_two, averaged


def unit_rates():
    blocks = FF // D
    fans = [2 * D // 3, 2 * D // 3, D, D // 64] + [D] * blocks + [FF] * blocks
    return [float(fan) ** -0.5 for fan in fans]


def update_kernel(
    owners, grad, masters, first, second, average, text_t, vec_grad, vec, vec_first, vec_second,
    vec_average,
    new_masters, new_first, new_second, new_average, new_copies, text_grad,
    vec_new_value, vec_new_first, vec_new_second, vec_new_average,
):
    n = lax.axis_index("narrow")
    owner, rank = unit_ranks(owners)
    for s in range(SLOTS):
        rate, filled = jnp.float32(0.0), jnp.int32(0)
        for u, value in enumerate(unit_rates()):
            match = (owner[u] == n) & (rank[u] == s)
            rate = rate + jnp.where(match, jnp.float32(value), jnp.float32(0.0))
            filled = filled + match.astype(jnp.int32)
        state = adam(
            masters[0, s], first[0, s], second[0, s], average[0, s], grad[s], rate
        )
        keep = jnp.broadcast_to(filled, state[0].shape) > 0
        state = [jnp.where(keep, part, 0.0) for part in state]
        for ref, part in zip((new_masters, new_first, new_second, new_average), state):
            ref[0, s] = part
        new_copies[0, s] = state[0].astype(BF16)
    text_grad[0] = text_t[...].T[0:LANG]
    state = adam(
        vec[...], vec_first[...], vec_second[...], vec_average[...], vec_grad[...], vector_rate
    )
    for ref, part in zip(
        (vec_new_value, vec_new_first, vec_new_second, vec_new_average), state
    ):
        ref[...] = part


def update(owners, grad, masters, first, second, average, text_t, vec_grad, vec, v1, v2, va):
    state = jax.ShapeDtypeStruct(masters.shape, F32)
    vector = jax.ShapeDtypeStruct((1, VEC), F32)
    return pl.pallas_call(
        update_kernel,
        out_shape=[state] * 4
        + [
            jax.ShapeDtypeStruct(masters.shape, BF16),
            jax.ShapeDtypeStruct((1, LANG, text_t.shape[0]), F32),
        ]
        + [vector] * 4,
        in_specs=[smem()] + [vmem()] * 11,
        out_specs=[vmem()] * 10,
        compiler_params=pltpu.CompilerParams(vmem_limit_bytes=VMEM_LIMIT),
    )(owners, grad, masters, first, second, average, text_t, vec_grad, vec, v1, v2, va)


def local(
    patches, text_tokens, view_counts, out_grad, owners, masters, first_moment, second_moment,
    average, vec_value, vec_first, vec_second, vec_average,
):
    vec = vec_value.reshape(1, VEC)
    units, text_t = gather(owners, masters, text_tokens)
    att_t, probs, inverse, q_t, keyed, v_t = attention_forward(
        view_counts, patches, text_t, vec, units
    )
    layer_out, middle_back, back_t, rest, gain_two, bias_two, up, down = dense(
        view_counts, att_t, patches, out_grad, vec, units
    )
    query_back, key_back, value_back = attention_backward(
        probs, inverse, keyed, v_t, back_t, q_t, att_t
    )
    patch_grad, first, gain_one, bias_one, text_part = project_back(
        patches, text_t, vec, units, middle_back, query_back, key_back, value_back
    )
    slot_grad, text_sum, vec_grad = reduce_all(
        owners, rest, first, text_part, (gain_one, bias_one, gain_two, bias_two, up, down)
    )
    outs = update(
        owners, slot_grad, masters, first_moment, second_moment, average, text_sum, vec_grad, vec,
        vec_first.reshape(1, VEC), vec_second.reshape(1, VEC), vec_average.reshape(1, VEC),
    )
    new_masters, new_first, new_second, new_average, new_copies, text_grad = outs[:6]
    vectors = [part.reshape(VEC) for part in outs[6:]]
    return (
        layer_out, patch_grad, text_grad, new_masters, new_first, new_second, new_average,
        new_copies, *vectors,
    )


def solution(mesh):
    rows = P(("wide", "narrow"), None)
    state = P("narrow", None, "wide", None)
    text = P("narrow", None, "wide")
    in_specs = (rows, text, rows, rows, P(), state, state, state, state, P(), P(), P(), P())
    out_specs = (rows, rows, text, state, state, state, state, state, P(), P(), P(), P())
    return jax.shard_map(local, mesh=mesh, in_specs=in_specs, out_specs=out_specs, check_vma=False)
```

time: 835 us -> 237 us (0.28); the launches traced: 822 us -> 236 us
  matrix products: 323 us -> 0 us
  waiting for transfers between devices: 322 us -> 0 us
  Pallas kernels: 0 us -> 224 us
  blocking collectives: 70.3 us -> 0 us
  local copies, waits for them, and re-layouts: 52.1 us -> 6.13 us
  other arithmetic: 37.8 us -> 5.49 us
  between operations: 15 us -> 0.71 us
    dot_general x141 -> x0, matrix products: 323 us -> none  [the longest x56 122 us: rmatmul(): lax.dot_general(left_side, right_side, (((1,), (1,)), ((), ())), preferre...]
    reduce_scatter x3 -> x0, waiting for transfers between devices: 249 us -> none  [the longest x1 193 us: local(): lax.psum_scatter(jnp.concatenate(pieces, axis=1), 'wide', scatter_dimensi...]
    pallas_call x0 -> x7, Pallas kernels: none -> 224 us  [the longest x1 60.2 us: reduce_all(): pl.pallas_call(reduce_kernel, out_shape=[jax.ShapeDtypeStruct((SLOTS, 64,...]
    all_gather x2 -> x0, waiting for transfers between devices: 73.2 us -> none  [the longest x1 53.7 us: local(): row_full = lax.all_gather(own_copy, 'wide', axis=2, tiled=True)]
    psum x1 -> x0, blocking collectives: 39.7 us -> none  [local(): vector_total = lax.psum(vector_grad, ('wide', 'narrow'))]
    all_gather x1 -> x0, blocking collectives: 30.5 us -> none  [local(): lax.all_gather(text_tokens, 'wide', axis=2, tiled=True)[0]]
    reduce_sum x28 -> x0, other arithmetic: 16 us -> none  [the longest x16 8.37 us: head_forward(): row_total = jnp.sum(patch_exp, axis=1) + jnp.sum(text_exp, axis=1)]
    convert_element_type x20 -> x0, other arithmetic: 15.5 us -> none  [the longest x8 8.25 us: head_backward(): (patch_prob * (patch_dprob - row_delta[:, None])).astype(jnp.bfloat16)]
  transfers between devices with their start and end apart: 5 -> 0, of which waited for: 4 -> 0; matrix products, arithmetic and copies ran while one was open for 5% -> 0% of each run, Pallas kernels for 0% -> 0%
where the time goes in v1:
time: 237 us; the launch traced here: 236 us
  Pallas kernels  224 us (95%)
  local copies, waits for them, and re-layouts  6.13 us (3%)
  other arithmetic  5.49 us (2%)
    pallas_call x1, Pallas kernels, reduce_all(): pl.pallas_call(reduce_kernel, out_shape=[jax.ShapeDtypeStruct((SLOTS, 64,...  60.2 us
    pallas_call x1, Pallas kernels, gather(): pl.pallas_call(gather_kernel, out_shape=[jax.ShapeDtypeStruct((UNITS, 4,...  50.8 us
    pallas_call x1, Pallas kernels, dense(): pl.pallas_call(functools.partial(dense_kernel, tile=tile), grid=(ROWS //...  33.6 us
    pallas_call x1, Pallas kernels, attention_backward(): pl.pallas_call(backward_kernel, grid=(4,), in_specs=[pl.BlockSpec((2, KEY...  33.1 us
    pallas_call x1, Pallas kernels, attention_forward(): pl.pallas_call(forward_kernel, grid=(4,), in_specs=[smem(), vmem(), vmem(...  32.2 us
    pallas_call x1, Pallas kernels, project_back(): pl.pallas_call(project_kernel, grid=(ROWS // tile,), in_specs=[rows, vmem...  10.6 us
    pallas_call x4, other arithmetic, update(): pl.pallas_call(update_kernel, out_shape=[state] * 4 + [jax.ShapeDtypeStru...  5.49 us

profile of v1, /device:TPU:0, one launch (start us, length us, event | category | flops | bytes accessed | tf_op | source)
XLA Modules:
  0.0 236.5 jit_solution(7704014211399282471)
XLA Ops:
  0.6 1.4 copy.25.text
  2.1 50.8 %shard_map.220 = (bf16[12,4,2,64,512]{4,3,2,1,0:T(8,128)(2,1)}, bf16[4,2,64,128]{3,2,1,0:T(8,128)(2,1)}) custom-call(s32[12]{0:T(128)} %owners.5, f32[1,4,64,512]{3,2,1,0:T(8,128)} %masters.3, bf16[1,77,64]{2,1,0:T(8,128)(2,1)} %copy.25.text), custom_call_target="tpu_custom_call" | custom-call | tf_op jit(solution)/shard_map/pallas_call | solution.py:213
  52.9 1.3 reshape.64.vec
  54.2 32.2 %shard_map.221 = (bf16[512,1280]{1,0:T(8,128)(2,1)}, bf16[8,1408,1280]{2,1,0:T(8,128)(2,1)}, f32[4,2,1280]{2,1,0:T(2,128)}, bf16[512,1280]{1,0:T(8,128)(2,1)}, b...) custom-call(s32[1,5]{1,0:T(1,128)} %counts.3, bf16[1280,512]{1,0:T(8,128)(2,1)} %x.5, bf16[512,128]{1,0:T(8,128)(2,1)} %bitcast.10, ...), custom_call_target="tpu_custom_call" | custom-call | tf_op jit(solution)/shard_map/pallas_call | solution.py:288
  86.4 33.6 %shard_map.222 = (bf16[1280,512]{1,0:T(8,128)(2,1)}, f32[1280,512]{1,0:T(8,128)}, bf16[512,1280]{1,0:T(8,128)(2,1)}, bf16[9,512,512]{2,1,0:T(8,128)(2,1)}, f32[1...) custom-call(s32[1,5]{1,0:T(1,128)} %counts.3, ...), custom_call_target="tpu_custom_call" | custom-call | tf_op jit(solution)/shard_map/pallas_call | solution.py:372
  120.0 33.1 %shard_map.223 = (bf16[512,1280]{1,0:T(8,128)(2,1)}, bf16[1408,512]{1,0:T(8,128)(2,1)}, bf16[1408,512]{1,0:T(8,128)(2,1)}) custom-call(bf16[8,1408,1280]{2,1,0:T(8,128)(2,1)} %get-tuple-element.54.probs, f32[4,2,1280]{2,1,0:T(2,128)} %get-tuple-element.55.inverse, bf16[4,1408,256]{2,1,0:T(8,128)(2,1)} %get-tuple-element.56.keyed, ...), custom_call_target="tpu_custom_call" | custom-call | tf_op jit(solution)/shard_map/pallas_call | solution.py:431
  153.1 10.6 %shard_map.224 = (f32[1280,512]{1,0:T(8,128)}, bf16[3,512,512]{2,1,0:T(8,128)(2,1)}, f32[1,512]{1,0:T(1,128)}, f32[1,512]{1,0:T(1,128)}, bf16[512,128]{1,0:T(8,128)(2,1)}) custom-call(bf16[1280,512]{1,0:T(8,128)(2,1)} %x.5, bf16[512,128]{1,0:T(8,128)(2,1)} %bitcast.11, f32[1,4608]{1,0:T(1,128)} %reshape.64.vec, bf16[12,512,512]{2,1,0:T(8,128)(2,1)} %bitcast.7, ...), custom_call_target="tpu_custom_call" | custom-call | tf_op jit(solution)/shard_map/pallas_call | solution.py:498
  163.7 0.0 copy-start
  163.7 0.0 copy-start.1
  163.7 0.0 copy-start.2
  163.7 60.2 %shard_map.225 = (f32[4,64,512]{2,1,0:T(8,128)}, f32[64,128]{1,0:T(8,128)}, f32[1,4608]{1,0:T(1,128)}) custom-call(s32[12]{0:T(128)} %owners.5, bf16[9,4,2,64,512]{4,3,2,1,0:T(8,128)(2,1)} %bitcast.8, bf16[3,4,2,64,512]{4,3,2,1,0:T(8,128)(2,1)} %bitcast.9, bf16[4,2,64,128]{3,2,1,0:T(8,128)(2,1)} %bitcast.12, f32[1,512]{1,0:T(1,128)} %get-tuple-element.67.gain_one, ...), custom_call_target="tpu_custom_call" | custom-call | tf_op jit(solution)/shard_map/pallas_call | solution.py:694
  223.9 0.0 copy-done
  223.9 0.6 reshape.69.vec_first
  224.5 0.0 copy-done.1
  224.5 0.6 reshape.70.vec_second
  225.1 0.0 copy-done.2
  225.1 0.6 reshape.71.vec_average
  225.8 3.8 %shard_map.226 = (f32[1,4,64,512]{3,2,1,0:T(8,128)}, f32[1,4,64,512]{3,2,1,0:T(8,128)}, f32[1,4,64,512]{3,2,1,0:T(8,128)}, f32[1,4,64,512]{3,2,1,0:T(8,128)}, bf...) custom-call(s32[12]{0:T(128)} %owners.5, ...), custom_call_target="tpu_custom_call" | custom-call | tf_op jit(solution)/shard_map/pallas_call | solution.py:791
  229.5 1.5 copy.26
  231.0 1.4 reduce
  232.4 1.4 reduce.1
  233.7 1.4 reduce.2
  235.1 1.4 reduce.3
Async XLA Ops:
  163.7 60.2 %copy-start = (f32[4608]{0:T(1024)S(1)}, f32[4608]{0:T(1024)}, u32[]{:S(2)}) copy-start(f32[4608]{0:T(1024)} %param.23) | copy-start | bytes 55300
  163.7 60.8 %copy-start.1 = (f32[4608]{0:T(1024)S(1)}, f32[4608]{0:T(1024)}, u32[]{:S(2)}) copy-start(f32[4608]{0:T(1024)} %param.24) | copy-start | bytes 55300
  163.7 61.4 %copy-start.2 = (f32[4608]{0:T(1024)S(1)}, f32[4608]{0:T(1024)}, u32[]{:S(2)}) copy-start(f32[4608]{0:T(1024)} %param.25) | copy-start | bytes 55300

commit v2 on v1

v2 whole, which is shorter than its diff:
```python
import functools

import jax
import jax.numpy as jnp
from jax import lax
from jax.experimental import pallas as pl
from jax.experimental.pallas import tpu as pltpu
from jax.sharding import PartitionSpec as P

D = 512
HEADS = 8
FF = 2048
VIEWS = 5
VIEW_ROWS = 256
ROWS = VIEWS * VIEW_ROWS
LANG = 77
TEXT = 128
KEYS = ROWS + TEXT
STEP = 5
UNITS = 12
SLOTS = 4
VEC = 5 * D + FF
F32 = jnp.float32
BF16 = jnp.bfloat16
MESH = pl.DeviceIdType.MESH
NEG = -1e30

norm_eps = 1e-05
beta_one = 0.5
beta_two = 0.5
adam_eps = 1e-08
weight_decay = 0.1
average_keep = 0.75
vector_rate = 0.25
VMEM_LIMIT = 60 * 2**20


def dot(left, right, left_dim=1, right_dim=0):
    return lax.dot_general(
        left, right, (((left_dim,), (right_dim,)), ((), ())), preferred_element_type=F32
    )


def vmem():
    return pl.BlockSpec(memory_space=pltpu.VMEM)


def smem():
    return pl.BlockSpec(memory_space=pltpu.SMEM)


def vec_row(vec, start, size):
    first = start // 128
    return jnp.concatenate([vec[first + r : first + r + 1, :] for r in range(size // 128)], axis=1)


def unit_ranks(owners_ref):
    owner = [owners_ref[u] for u in range(UNITS)]
    rank = []
    for u in range(UNITS):
        total = jnp.int32(0)
        for v in range(u):
            total = total + (owner[v] == owner[u]).astype(jnp.int32)
        rank.append(jnp.minimum(total, SLOTS - 1))
    return owner, rank


def normalize(values):
    center = values - jnp.mean(values, axis=-1, keepdims=True)
    spread = jnp.mean(center * center, axis=-1, keepdims=True)
    scale = lax.rsqrt(spread + norm_eps)
    return center * scale, scale


def norm_back(grads, gain, normed, scale):
    e = grads * gain
    return scale * (
        e
        - jnp.mean(e, axis=-1, keepdims=True)
        - normed * jnp.mean(e * normed, axis=-1, keepdims=True)
    )


def place():
    w = lax.axis_index("wide")
    n = lax.axis_index("narrow")
    return w, n, w // 2, w % 2, n // 2, n % 2


def narrow_peers(w, n):
    return [(w, lax.rem(n + k, 4)) for k in range(1, 4)]


def wide_peers(w, n):
    return [(lax.rem(w + k, 8), n) for k in range(1, 8)]


def greet(peers):
    barrier = pltpu.get_barrier_semaphore()
    for peer in peers:
        pl.semaphore_signal(barrier, inc=1, device_id=peer, device_id_type=MESH)


def greeted(peers):
    pl.semaphore_wait(pltpu.get_barrier_semaphore(), len(peers))


class Links:
    def __init__(self, send, recv):
        self.send, self.recv, self.slots = send, recv, {}

    def copies(self, key, parts):
        made = []
        for k, (src, dst, device) in enumerate(parts()):
            slot = self.slots.setdefault((key, k), len(self.slots))
            made.append(
                pltpu.make_async_remote_copy(
                    src_ref=src,
                    dst_ref=dst,
                    send_sem=self.send.at[slot],
                    recv_sem=self.recv.at[slot],
                    device_id=device,
                    device_id_type=MESH,
                )
            )
        return made

    def start(self, key, parts):
        for copy in self.copies(key, parts):
            copy.start()

    def wait(self, key, parts):
        for copy in self.copies(key, parts):
            copy.wait()


def partners(w, n, z, x, y, c):
    to_z = [(lax.rem(z + k, 4) * 2 + x, n) for k in range(1, 4)]
    return to_z, (z * 2 + 1 - x, n), (w, (1 - y) * 2 + c), (w, y * 2 + 1 - c)


def spread(ref, head, own, stage, at):
    w, n, z, x, y, c = at
    to_z, to_x, to_y, to_c = partners(*at)
    if stage == 0:
        return [(own, ref.at[(*head, z, x, y, c)], peer) for peer in to_z]
    if stage == 1:
        parts = [((pl.ds(0, 2), x, y, c), to_x), ((pl.ds(2, 2), x, y, c), to_y)]
    elif stage == 2:
        whole = slice(None)
        parts = [((pl.ds(0, 2), whole, y, c), to_y), ((pl.ds(2, 2), x, whole, c), to_x)]
    else:
        whole = slice(None)
        parts = [((whole, whole, whole, c), to_c)]
    return [(ref.at[(*head, *part)], ref.at[(*head, *part)], peer) for part, peer in parts]


def front_kernel(
    owners, counts, masters, text, x, vec,
    att_t, probs, inverse, q_out, key_out, v_out, normed_out, w_first_out, w_rest, text_out,
    send_buf, slot_buf, own, w_first, text_buf, q_t, keyed, v_t, normed, normed_t, text_normed,
    send, recv, local
):
    i = pl.program_id(0)
    at = place()
    w, n, z, sx, y, c = at
    links = Links(send, recv)
    rest_own = pltpu.make_async_copy(
        own.at[pl.ds(3, 9)], w_rest.at[:, z, sx, y, c], local.at[0]
    )
    written = [
        pltpu.make_async_copy(q_t, q_out, local.at[1]),
        pltpu.make_async_copy(keyed.at[:, :, pl.ds(0, 128)], key_out, local.at[2]),
        pltpu.make_async_copy(v_t, v_out, local.at[3]),
        pltpu.make_async_copy(normed_t, normed_out, local.at[4]),
        pltpu.make_async_copy(w_first, w_first_out, local.at[5]),
        pltpu.make_async_copy(text_buf, text_out, local.at[6]),
    ]

    def rest(g, stage):
        head = (pl.ds(3 * g, 3),)
        return ("rest", g, stage), lambda: spread(
            w_rest, head, own.at[pl.ds(3 + 3 * g, 3)], stage, at
        )

    @pl.when(i == 0)
    def _():
        peers = narrow_peers(w, n) + wide_peers(w, n)
        greet(peers)
        send_buf[...] = masters[0].reshape(SLOTS, 4, 16, D).astype(BF16)
        text_buf[z, sx] = jnp.zeros((64, TEXT), BF16)
        text_buf[z, sx, :, 0:LANG] = text[0]
        greeted(peers)
        slots = "slots", lambda: [
            (send_buf.at[:, q], slot_buf.at[n], (w, q)) for _, q in narrow_peers(w, n)
        ]
        links.start(*slots)
        piece = text_buf.at[z, sx]
        texts = "text", lambda: [(piece, piece, peer) for peer in wide_peers(w, n)]
        links.start(*texts)
        slot_buf[n] = send_buf[:, n]
        gain, bias = vec_row(vec, 0, D), vec_row(vec, D, D)
        low = (normalize(x[...].astype(F32))[0] * gain + bias).astype(BF16)
        normed[...] = low
        owner, rank = unit_ranks(owners)
        links.wait(*slots)
        for u in range(UNITS):
            own[u] = slot_buf[owner[u], rank[u]]
        for u in range(3):
            w_first[u, z, sx, y, c] = own[u]

        order = (1, 0, 2)

        def first(u, s):
            return ("first", u, s), lambda: spread(w_first, (u,), own.at[u], s, at)

        for u in order:
            links.start(*first(u, 0))
        rest_own.start()
        normed_t[:, 0:ROWS] = normed[...].astype(F32).T.astype(BF16)
        links.wait(*texts)
        live_text = lax.broadcasted_iota(jnp.int32, (TEXT, 1), 0) < LANG
        rows = text_buf[...].reshape(D, TEXT).astype(F32).T
        text_low = jnp.where(live_text, normalize(rows)[0] * gain + bias, 0.0)
        text_normed[...] = text_low.astype(BF16)
        normed_t[:, ROWS:KEYS] = text_low.T.astype(BF16)
        for p in range(4):
            for v, live in enumerate(live_column(counts, ROWS)):
                keyed[p, v * VIEW_ROWS : (v + 1) * VIEW_ROWS, 128:256] = jnp.broadcast_to(
                    jnp.where(live, 0.0, NEG), (VIEW_ROWS, 128)
                ).astype(BF16)
            keyed[p, ROWS:KEYS, 128:256] = jnp.broadcast_to(
                jnp.where(live_text, 0.0, NEG), (TEXT, 128)
            ).astype(BF16)

        def unit(u):
            return w_first[u].reshape(D, D)

        def project(u):
            if u == 1:
                k = dot(normed[...], unit(1)).astype(BF16)
                t = dot(text_normed[...], unit(1)).astype(BF16)
                for p in range(4):
                    pair = slice(p * 128, (p + 1) * 128)
                    keyed[p, 0:ROWS, 0:128] = k[:, pair]
                    keyed[p, ROWS:KEYS, 0:128] = t[:, pair]
            elif u == 0:
                q_t[...] = dot(unit(0), normed[...], 0, 1).astype(BF16) * BF16(0.125)
            else:
                v_t[:, 0:ROWS] = dot(unit(2), normed[...], 0, 1).astype(BF16)
                v_t[:, ROWS:KEYS] = dot(unit(2), text_normed[...], 0, 1).astype(BF16)

        for step in range(3 + 3):
            for s in (3, 2, 1, 0):
                g = step - s
                if not 0 <= g < 3:
                    continue
                u = order[g]
                links.wait(*first(u, s))
                if s < 3:
                    links.start(*first(u, s + 1))
                if (g, s) == (2, 0):
                    links.start(*rest(0, 0))
                if (g, s) == (2, 1):
                    links.start(*rest(1, 0))
                if (g, s) == (2, 2):
                    links.start(*rest(2, 0))
                if s == 3:
                    project(u)
        for copy in written:
            copy.start()

    plan = {
        0: ["local", (0, 0)], 1: [(1, 0)], 2: [(2, 0), (0, 1)], 3: [(1, 1)],
        4: [(2, 1), (0, 2)], 5: [(1, 2)], 6: [(2, 2), (0, 3)], 7: [(1, 3)],
    }

    def comm(t):
        for item in plan[t]:
            if item == "local":
                rest_own.wait()
                continue
            g, s = item
            links.wait(*rest(g, s))
            if s < 3:
                links.start(*rest(g, s + 1))

    row = lax.broadcasted_iota(jnp.int32, (128, ROWS), 0)
    one = jnp.where(row == 0, 1.0, 0.0).astype(BF16)
    for h in range(2):
        for k in range(4):
            pl.when(i == k)(functools.partial(comm, 2 * k + h))
        pair_q = q_t[pl.ds(pl.multiple_of(i * 128, 128), 128), :]
        mine = (row >= 64 * h) & (row < 64 * h + 64)
        q = jnp.where(mine, pair_q, jnp.zeros_like(pair_q))
        scores = dot(keyed[i], jnp.concatenate([q, one], axis=0))
        peak = jnp.max(scores, axis=0, keepdims=True)
        e = jnp.exp(scores - peak)
        total = jnp.sum(e, axis=0, keepdims=True)
        low = e.astype(BF16)
        probs[h] = low
        mixed = dot(v_t[pl.ds(pl.multiple_of(i * 128 + h * 64, 64), 64), :], low)
        inv = 1.0 / total
        att_t[h * 64 : (h + 1) * 64, :] = (mixed * inv).astype(BF16)
        inverse[0, h : h + 1, :] = inv

    @pl.when(i == 3)
    def _():
        links.wait(*rest(2, 3))
        for copy in written:
            copy.wait()


def front(owners, counts, masters, text, x, vec):
    hbm = pl.BlockSpec(memory_space=pl.ANY)
    copies = 3 + 7 + 3 * 8 + 3 * 8
    return pl.pallas_call(
        front_kernel,
        grid=(4,),
        in_specs=[smem(), smem(), vmem(), vmem(), vmem(), vmem()],
        out_specs=[
            pl.BlockSpec((128, ROWS), lambda i: (i, 0)),
            pl.BlockSpec((2, KEYS, ROWS), lambda i: (i, 0, 0)),
            pl.BlockSpec((1, 2, ROWS), lambda i: (i, 0, 0)),
        ]
        + [hbm] * 7,
        out_shape=[
            jax.ShapeDtypeStruct((D, ROWS), BF16),
            jax.ShapeDtypeStruct((HEADS, KEYS, ROWS), BF16),
            jax.ShapeDtypeStruct((4, 2, ROWS), F32),
            jax.ShapeDtypeStruct((D, ROWS), BF16),
            jax.ShapeDtypeStruct((4, KEYS, 128), BF16),
            jax.ShapeDtypeStruct((D, KEYS), BF16),
            jax.ShapeDtypeStruct((D, KEYS), BF16),
            jax.ShapeDtypeStruct((3, 4, 2, 2, 2, 16, D), BF16),
            jax.ShapeDtypeStruct((9, 4, 2, 2, 2, 16, D), BF16),
            jax.ShapeDtypeStruct((4, 2, 64, TEXT), BF16),
        ],
        scratch_shapes=[
            pltpu.VMEM((SLOTS, 4, 16, D), BF16),
            pltpu.VMEM((4, SLOTS, 16, D), BF16),
            pltpu.VMEM((UNITS, 16, D), BF16),
            pltpu.VMEM((3, 4, 2, 2, 2, 16, D), BF16),
            pltpu.VMEM((4, 2, 64, TEXT), BF16),
            pltpu.VMEM((D, ROWS), BF16),
            pltpu.VMEM((4, KEYS, 256), BF16),
            pltpu.VMEM((D, KEYS), BF16),
            pltpu.VMEM((ROWS, D), BF16),
            pltpu.VMEM((D, KEYS), BF16),
            pltpu.VMEM((TEXT, D), BF16),
            pltpu.SemaphoreType.DMA((copies,)),
            pltpu.SemaphoreType.DMA((copies,)),
            pltpu.SemaphoreType.DMA((7,)),
        ],
        compiler_params=pltpu.CompilerParams(
            collective_id=1, has_side_effects=True, vmem_limit_bytes=VMEM_LIMIT
        ),
    )(owners, counts, masters, text, x, vec)


def gather(owners, masters, text_t):
    packed = lax.all_gather(masters.astype(BF16), "wide", axis=2, tiled=True)
    packed = lax.all_gather(packed, "narrow", axis=0, tiled=True)
    same = owners[:, None] == owners[None, :]
    ids = jnp.arange(UNITS)
    rank = jnp.sum((same & (ids[None, :] < ids[:, None])).astype(jnp.int32), axis=1)
    units = jnp.take(packed.reshape(-1, D, D), owners * SLOTS + rank, axis=0)
    rows = lax.all_gather(text_t, "wide", axis=1, tiled=True)[0]
    return units, jnp.pad(rows, ((0, 0), (0, TEXT - LANG)))


def live_column(counts, rows):
    index = lax.broadcasted_iota(jnp.int32, (VIEW_ROWS, 1), 0)
    return [(index < counts[0, v]) for v in range(rows // VIEW_ROWS)]


def forward_kernel(
    counts, x, text_t, vec, w, att_t, probs, inverse, q_t, keyed, v_t, normed, text_normed
):
    i = pl.program_id(0)

    @pl.when(i == 0)
    def _():
        gain, bias = vec_row(vec, 0, D), vec_row(vec, D, D)
        normed[...] = (normalize(x[...].astype(F32))[0] * gain + bias).astype(BF16)
        rows = text_t[...].astype(F32).T
        live_text = lax.broadcasted_iota(jnp.int32, (TEXT, 1), 0) < LANG
        text_normed[...] = jnp.where(
            live_text, normalize(rows)[0] * gain + bias, 0.0
        ).astype(BF16)
        q_t[...] = dot(w[0], normed[...], 0, 1).astype(BF16) * BF16(0.125)
        v_t[:, 0:ROWS] = dot(w[2], normed[...], 0, 1).astype(BF16)
        v_t[:, ROWS:KEYS] = dot(w[2], text_normed[...], 0, 1).astype(BF16)
        for p in range(4):
            pair = slice(p * 128, (p + 1) * 128)
            keyed[p, 0:ROWS, 0:128] = dot(normed[...], w[1, :, pair]).astype(BF16)
            keyed[p, ROWS:KEYS, 0:128] = dot(text_normed[...], w[1, :, pair]).astype(BF16)
            for v, live in enumerate(live_column(counts, ROWS)):
                keyed[p, v * VIEW_ROWS : (v + 1) * VIEW_ROWS, 128:256] = jnp.broadcast_to(
                    jnp.where(live, 0.0, NEG), (VIEW_ROWS, 128)
                ).astype(BF16)
            keyed[p, ROWS:KEYS, 128:256] = jnp.broadcast_to(
                jnp.where(live_text, 0.0, NEG), (TEXT, 128)
            ).astype(BF16)

    row = lax.broadcasted_iota(jnp.int32, (128, ROWS), 0)
    one = jnp.where(row == 0, 1.0, 0.0).astype(BF16)
    pair_q = q_t[pl.ds(pl.multiple_of(i * 128, 128), 128), :]
    for h in range(2):
        mine = (row >= 64 * h) & (row < 64 * h + 64)
        q = jnp.where(mine, pair_q, jnp.zeros_like(pair_q))
        scores = dot(keyed[i], jnp.concatenate([q, one], axis=0))
        peak = jnp.max(scores, axis=0, keepdims=True)
        e = jnp.exp(scores - peak)
        total = jnp.sum(e, axis=0, keepdims=True)
        low = e.astype(BF16)
        probs[h] = low
        mixed = dot(v_t[pl.ds(pl.multiple_of(i * 128 + h * 64, 64), 64), :], low)
        inv = 1.0 / total
        att_t[h * 64 : (h + 1) * 64, :] = (mixed * inv).astype(BF16)
        inverse[0, h : h + 1, :] = inv


def attention_forward(counts, x, text_t, vec, units):
    return pl.pallas_call(
        forward_kernel,
        grid=(4,),
        in_specs=[smem(), vmem(), vmem(), vmem(), pl.BlockSpec((3, D, D), lambda i: (0, 0, 0))],
        out_specs=[
            pl.BlockSpec((128, ROWS), lambda i: (i, 0)),
            pl.BlockSpec((2, KEYS, ROWS), lambda i: (i, 0, 0)),
            pl.BlockSpec((1, 2, ROWS), lambda i: (i, 0, 0)),
            pl.BlockSpec((D, ROWS), lambda i: (0, 0)),
            pl.BlockSpec((4, KEYS, 256), lambda i: (0, 0, 0)),
            pl.BlockSpec((D, KEYS), lambda i: (0, 0)),
        ],
        out_shape=[
            jax.ShapeDtypeStruct((D, ROWS), BF16),
            jax.ShapeDtypeStruct((HEADS, KEYS, ROWS), BF16),
            jax.ShapeDtypeStruct((4, 2, ROWS), F32),
            jax.ShapeDtypeStruct((D, ROWS), BF16),
            jax.ShapeDtypeStruct((4, KEYS, 256), BF16),
            jax.ShapeDtypeStruct((D, KEYS), BF16),
        ],
        scratch_shapes=[pltpu.VMEM((ROWS, D), BF16), pltpu.VMEM((TEXT, D), BF16)],
        compiler_params=pltpu.CompilerParams(vmem_limit_bytes=VMEM_LIMIT),
    )(counts, x, text_t, vec, units)


def dense_kernel(
    counts, att_t, x, g, vec, w,
    layer_out, middle_back, back_t, grads, gain_grad, bias_grad, up_grad, down_grad,
    total, *, tile
):
    i = pl.program_id(0)
    steps = pl.num_programs(0)
    gain, bias = vec_row(vec, 2 * D, D), vec_row(vec, 3 * D, D)
    a = att_t[...]
    index = lax.broadcasted_iota(jnp.int32, (tile, 1), 0) + i * tile
    live = jnp.zeros((tile, 1), jnp.bool_)
    for v in range(VIEWS):
        live = live | ((index >= v * VIEW_ROWS) & (index < v * VIEW_ROWS + counts[0, v]))
    middle = x[...].astype(F32) + dot(a, w[0], 0, 0)
    normed, scale = normalize(middle)
    low = (normed * gain + bias).astype(BF16)
    out_back = jnp.where(live, g[...].astype(F32), 0.0)
    out_low = out_back.astype(BF16)

    @pl.when(i == 0)
    def _():
        total[...] = jnp.zeros_like(total)
        gain_grad[...] = jnp.zeros_like(gain_grad)
        bias_grad[...] = jnp.zeros_like(bias_grad)
        up_grad[...] = jnp.zeros_like(up_grad)
        down_grad[...] = jnp.zeros_like(down_grad)

    out = middle + vec_row(vec, 4 * D + FF, D)
    normed_back = jnp.zeros((tile, D), F32)
    for j in range(4):
        block = slice(j * D, (j + 1) * D)
        preact = dot(low, w[1 + j]) + vec_row(vec, 4 * D + j * D, D)
        phi = 0.5 + 0.5 * lax.erf(preact * 0.7071067811865476)
        active = (preact * phi).astype(BF16)
        slope = phi + preact * (jnp.exp(-0.5 * preact * preact) * 0.3989422804014327)
        out = out + dot(active, w[5 + j])
        preact_back = (dot(out_low, w[5 + j], 1, 1) * slope).astype(BF16)
        normed_back = normed_back + dot(preact_back, w[1 + j], 1, 1)
        total[1 + j] += dot(low, preact_back, 0, 0)
        total[5 + j] += dot(active, out_low, 0, 0)
        up_grad[:, block] += jnp.sum(preact_back.astype(F32), axis=0, keepdims=True)
    layer_out[...] = jnp.where(live, out, 0.0).astype(BF16)
    back = out_back + norm_back(normed_back, gain, normed, scale)
    middle_back[...] = back
    branch = back.astype(BF16)
    back_t[...] = dot(w[0], branch, 1, 1).astype(BF16)
    total[0] += dot(a, branch)
    gain_grad[...] += jnp.sum(normed_back * normed, axis=0, keepdims=True)
    bias_grad[...] += jnp.sum(normed_back, axis=0, keepdims=True)
    down_grad[...] += jnp.sum(out_back, axis=0, keepdims=True)

    @pl.when(i == steps - 1)
    def _():
        grads[...] = total[...].astype(BF16)


def dense(counts, att_t, x, g, vec, units, tile=640):
    rows = pl.BlockSpec((tile, D), lambda i: (i, 0))
    columns = pl.BlockSpec((D, tile), lambda i: (0, i))
    return pl.pallas_call(
        functools.partial(dense_kernel, tile=tile),
        grid=(ROWS // tile,),
        in_specs=[smem(), columns, rows, rows, vmem(), vmem()],
        out_specs=[
            rows,
            rows,
            columns,
            pl.BlockSpec((9, D, D), lambda i: (0, 0, 0)),
            pl.BlockSpec((1, D), lambda i: (0, 0)),
            pl.BlockSpec((1, D), lambda i: (0, 0)),
            pl.BlockSpec((1, FF), lambda i: (0, 0)),
            pl.BlockSpec((1, D), lambda i: (0, 0)),
        ],
        out_shape=[
            jax.ShapeDtypeStruct((ROWS, D), BF16),
            jax.ShapeDtypeStruct((ROWS, D), F32),
            jax.ShapeDtypeStruct((D, ROWS), BF16),
            jax.ShapeDtypeStruct((9, D, D), BF16),
            jax.ShapeDtypeStruct((1, D), F32),
            jax.ShapeDtypeStruct((1, D), F32),
            jax.ShapeDtypeStruct((1, FF), F32),
            jax.ShapeDtypeStruct((1, D), F32),
        ],
        scratch_shapes=[pltpu.VMEM((9, D, D), F32)],
        compiler_params=pltpu.CompilerParams(vmem_limit_bytes=VMEM_LIMIT),
    )(counts, att_t, x, g, vec, units)


def backward_kernel(probs, inverse, keyed, v_t, back_t, q_t, att_t, query_back, key_back, value_back):
    row = lax.broadcasted_iota(jnp.int32, (128, ROWS), 0)
    lane = lax.broadcasted_iota(jnp.int32, (KEYS, 128), 1)
    ones = jnp.where(lane < 2, 1.0, 0.0).astype(BF16)
    value = jnp.concatenate([v_t[...].astype(F32).T.astype(BF16), ones], axis=1)
    key_t = keyed[:, 0:128].astype(F32).T.astype(BF16)
    back = back_t[...].astype(F32)
    product = back * att_t[...].astype(F32)
    query = q_t[...].astype(F32)
    key_total = jnp.zeros((KEYS, 128), F32)
    value_total = jnp.zeros((KEYS, 128), F32)
    for h in range(2):
        half = slice(h * 64, (h + 1) * 64)
        inv = inverse[0, h : h + 1, :]
        delta = jnp.sum(product[half], axis=0, keepdims=True) * inv
        high = delta.astype(BF16).astype(F32)
        mine = (row >= 64 * h) & (row < 64 * h + 64)
        scaled = jnp.where(mine, back * inv, 0.0)
        tail = jnp.where(row == 0, -high, jnp.where(row == 1, high - delta, 0.0))
        right = jnp.concatenate([scaled.astype(BF16), tail.astype(BF16)], axis=0)
        low = probs[h]
        score_back = low * dot(value, right).astype(BF16)
        query_back[half, :] = (dot(key_t[half], score_back) * 0.125).astype(BF16)
        key_total += dot(score_back, jnp.where(mine, query, 0.0).T.astype(BF16))
        value_total += dot(low, scaled.T.astype(BF16))
    key_back[...] = key_total.astype(BF16)
    value_back[...] = value_total.astype(BF16)


def attention_backward(probs, inverse, keyed, v_t, back_t, q_t, att_t):
    return pl.pallas_call(
        backward_kernel,
        grid=(4,),
        in_specs=[
            pl.BlockSpec((2, KEYS, ROWS), lambda i: (i, 0, 0)),
            pl.BlockSpec((1, 2, ROWS), lambda i: (i, 0, 0)),
            pl.BlockSpec((None, KEYS, 256), lambda i: (i, 0, 0)),
            pl.BlockSpec((128, KEYS), lambda i: (i, 0)),
            pl.BlockSpec((128, ROWS), lambda i: (i, 0)),
            pl.BlockSpec((128, ROWS), lambda i: (i, 0)),
            pl.BlockSpec((128, ROWS), lambda i: (i, 0)),
        ],
        out_specs=[
            pl.BlockSpec((128, ROWS), lambda i: (i, 0)),
            pl.BlockSpec((KEYS, 128), lambda i: (0, i)),
            pl.BlockSpec((KEYS, 128), lambda i: (0, i)),
        ],
        out_shape=[
            jax.ShapeDtypeStruct((D, ROWS), BF16),
            jax.ShapeDtypeStruct((KEYS, D), BF16),
            jax.ShapeDtypeStruct((KEYS, D), BF16),
        ],
        compiler_params=pltpu.CompilerParams(vmem_limit_bytes=VMEM_LIMIT),
    )(probs, inverse, keyed, v_t, back_t, q_t, att_t)


def project_kernel(
    x, text_t, vec, w, middle_back, query_back, key_back, value_back, text_key, text_value,
    patch_grad, grads, gain_grad, bias_grad, text_grad_t, total
):
    i = pl.program_id(0)
    steps = pl.num_programs(0)
    gain, bias = vec_row(vec, 0, D), vec_row(vec, D, D)

    @pl.when(i == 0)
    def _():
        live = lax.broadcasted_iota(jnp.int32, (TEXT, 1), 0) < LANG
        normed, scale = normalize(text_t[...].astype(F32).T)
        low_t = jnp.where(live, normed * gain + bias, 0.0).T.astype(BF16)
        k, v = text_key[...], text_value[...]
        back = dot(k, w[1], 1, 1) + dot(v, w[2], 1, 1)
        text_grad_t[...] = norm_back(back, gain, normed, scale).T.astype(BF16)
        gain_grad[...] = jnp.sum(back * normed, axis=0, keepdims=True)
        bias_grad[...] = jnp.sum(back, axis=0, keepdims=True)
        total[0] = jnp.zeros((D, D), F32)
        total[1] = dot(low_t, k)
        total[2] = dot(low_t, v)

    normed, scale = normalize(x[...].astype(F32))
    low_t = (normed * gain + bias).T.astype(BF16)
    q, k, v = query_back[...], key_back[...], value_back[...]
    back = dot(q, w[0], 0, 1) + dot(k, w[1], 1, 1) + dot(v, w[2], 1, 1)
    patch_grad[...] = middle_back[...] + norm_back(back, gain, normed, scale)
    total[0] += dot(low_t, q, 1, 1)
    total[1] += dot(low_t, k)
    total[2] += dot(low_t, v)
    gain_grad[...] += jnp.sum(back * normed, axis=0, keepdims=True)
    bias_grad[...] += jnp.sum(back, axis=0, keepdims=True)

    @pl.when(i == steps - 1)
    def _():
        grads[...] = total[...].astype(BF16)


def project_back(x, text_t, vec, units, middle_back, query_back, key_back, value_back, tile=640):
    rows = pl.BlockSpec((tile, D), lambda i: (i, 0))
    text_rows = pl.BlockSpec((TEXT, D), lambda i: (ROWS // TEXT, 0))
    return pl.pallas_call(
        project_kernel,
        grid=(ROWS // tile,),
        in_specs=[
            rows,
            vmem(),
            vmem(),
            pl.BlockSpec((3, D, D), lambda i: (0, 0, 0)),
            rows,
            pl.BlockSpec((D, tile), lambda i: (0, i)),
            rows,
            rows,
            text_rows,
            text_rows,
        ],
        out_specs=[
            rows,
            pl.BlockSpec((3, D, D), lambda i: (0, 0, 0)),
            pl.BlockSpec((1, D), lambda i: (0, 0)),
            pl.BlockSpec((1, D), lambda i: (0, 0)),
            pl.BlockSpec((D, TEXT), lambda i: (0, 0)),
        ],
        out_shape=[
            jax.ShapeDtypeStruct((ROWS, D), F32),
            jax.ShapeDtypeStruct((3, D, D), BF16),
            jax.ShapeDtypeStruct((1, D), F32),
            jax.ShapeDtypeStruct((1, D), F32),
            jax.ShapeDtypeStruct((D, TEXT), BF16),
        ],
        scratch_shapes=[pltpu.VMEM((3, D, D), F32)],
        compiler_params=pltpu.CompilerParams(vmem_limit_bytes=VMEM_LIMIT),
    )(
        x, text_t, vec, units, middle_back, query_back, key_back, value_back, key_back, value_back
    )


def add(a, b):
    return (a.astype(F32) + b.astype(F32)).astype(BF16)


class Reducer:
    def __init__(self, name, links, at, source, kept, bufs):
        self.name, self.links, self.at = name, links, at
        self.source, self.kept = source, kept
        (self.c_buf, self.ya_buf, self.xb_buf, self.xa_buf, self.yb_buf, self.z_sum,
         self.z_buf) = bufs

    def start(self, stage, head):
        self.links.start(*self.copies(stage, head))

    def copies(self, stage, head):
        return (self.name, str(head), stage), lambda: self.parts(stage, head)

    def parts(self, stage, head):
        w, n, z, x, y, c = self.at
        to_z, to_x, to_y, to_c = partners(*self.at)
        whole = slice(None)
        if stage == 0:
            return [(self.source.at[(*head, whole, whole, whole, 1 - c)], self.c_buf.at[head], to_c)]
        elif stage == 1:
            return [
                (self.kept.at[(*head, pl.ds(0, 2), whole, 1 - y)], self.ya_buf.at[head], to_y),
                (self.kept.at[(*head, pl.ds(2, 2), 1 - x)], self.xb_buf.at[head], to_x),
            ]
        elif stage == 2:
            return [
                (self.kept.at[(*head, pl.ds(0, 2), 1 - x, y)], self.xa_buf.at[head], to_x),
                (self.kept.at[(*head, pl.ds(2, 2), x, 1 - y)], self.yb_buf.at[head], to_y),
            ]
        else:
            return [
                (self.z_sum.at[(*head, lax.rem(z + k, 4))], self.z_buf.at[(k - 1, *head)],
                 to_z[k - 1])
                for k in range(1, 4)
            ]
    def finish(self, stage, head):
        w, n, z, x, y, c = self.at
        self.links.wait(*self.copies(stage, head))
        kept = self.kept
        low, high = pl.ds(0, 2), pl.ds(2, 2)
        whole = slice(None)
        if stage == 0:
            kept[head] = add(kept[head], self.c_buf[head])
        elif stage == 1:
            a = (*head, low, whole, y)
            b = (*head, high, x)
            kept[a] = add(kept[a], self.ya_buf[head])
            kept[b] = add(kept[b], self.xb_buf[head])
        elif stage == 2:
            self.z_sum[(*head, low)] = add(kept[(*head, low, x, y)], self.xa_buf[head])
            self.z_sum[(*head, high)] = add(kept[(*head, high, x, y)], self.yb_buf[head])
        else:
            total = self.z_sum[(*head, z)].astype(F32)
            for k in range(3):
                total = total + self.z_buf[(k, *head)].astype(F32)
            return total.astype(BF16)


def reducer_scratch(lead, columns):
    shapes = [(4, 2, 2), (2, 2), (2, 2), (2,), (2,), (4,)]
    bufs = [pltpu.VMEM((*lead, *shape, 16, columns), BF16) for shape in shapes]
    return bufs + [pltpu.VMEM((3, *lead, 16, columns), BF16)]


def back_kernel(
    owners, probs, inverse, keyed, v_t, back_t, q_t, att_t, normed_t, rest, w_first, text_t, x,
    middle_back, vec, gain_two, bias_two, up, down,
    patch_grad, slot_grad, text_out, vec_out,
    rest_kept, *scratch
):
    rest_bufs, scratch = scratch[:7], scratch[7:]
    first_bufs, scratch = scratch[:7], scratch[7:]
    (first_all, first_kept, red, s_buf, r_buf, text_part, text_buf, v_own, vw_buf, v_sum, vn_buf,
     query_back, key_back, value_back, x_buf, middle_buf, patch_buf, send, recv, local) = scratch
    i = pl.program_id(0)
    at = place()
    w, n, z, sx, y, c = at
    links = Links(send, recv)
    whole = slice(None)
    rest_red = Reducer("rest", links, at, rest, rest_kept, rest_bufs)
    first_red = Reducer("first", links, at, first_all, first_kept, first_bufs)
    groups = [(pl.ds(3 * g, 3),) for g in range(3)]
    chunks = [(p, whole) for p in range(4)]
    read = [
        pltpu.make_async_copy(
            rest.at[:, :, :, :, c], rest_kept, local.at[0]
        ),
        pltpu.make_async_copy(x, x_buf, local.at[1]),
        pltpu.make_async_copy(middle_back, middle_buf, local.at[2]),
    ]
    write = pltpu.make_async_copy(patch_buf, patch_grad, local.at[3])

    def step_first(p, stage):
        total = first_red.finish(stage, chunks[p])
        if stage < 3:
            first_red.start(stage + 1, chunks[p])
        else:
            red[0:3, :, p * 128 : (p + 1) * 128] = total

    def step_rest(g, stage):
        total = rest_red.finish(stage, groups[g])
        if stage < 3:
            rest_red.start(stage + 1, groups[g])
        else:
            red[3 + 3 * g : 6 + 3 * g] = total

    plan = {
        0: [], 1: [(0, 0)], 2: [(1, 0)], 3: [(2, 0), (0, 1)], 4: [(1, 1)], 5: [(2, 1), (0, 2)],
        6: [(1, 2)], 7: [(2, 2), (0, 3)],
    }
    first_plan = {3: [(0, 0)], 4: [(0, 1)], 5: [(1, 0), (0, 2)], 6: [(1, 1), (0, 3)],
                  7: [(2, 0), (1, 2)]}

    def comm(t):
        if t == 0:
            for copy in read:
                copy.start()
            peers = narrow_peers(w, n) + wide_peers(w, n)
            greet(peers)
            offset = 4 * 2
            for piece in (gain_two, bias_two, up, down):
                for r in range(piece.shape[1] // 128):
                    v_own[offset : offset + 1, :] = piece[:, r * 128 : (r + 1) * 128]
                    offset += 1
            greeted(peers)
            for g in range(3):
                rest_red.start(0, groups[g])
            read[0].wait()
        for g, s in plan[t]:
            step_rest(g, s)
        for p, s in first_plan.get(t, []):
            step_first(p, s)

    row = lax.broadcasted_iota(jnp.int32, (128, ROWS), 0)
    lane = lax.broadcasted_iota(jnp.int32, (KEYS, 128), 1)
    ones = jnp.where(lane < 2, 1.0, 0.0).astype(BF16)
    value = jnp.concatenate([v_t[...].astype(F32).T.astype(BF16), ones], axis=1)
    key_t = keyed[...].astype(F32).T.astype(BF16)
    back = back_t[...].astype(F32)
    product = back * att_t[...].astype(F32)
    query = q_t[...].astype(F32)
    key_total = jnp.zeros((KEYS, 128), F32)
    value_total = jnp.zeros((KEYS, 128), F32)
    query_parts = []
    for h in range(2):
        for k in range(4):
            pl.when(i == k)(functools.partial(comm, 2 * k + h))
        half = slice(h * 64, (h + 1) * 64)
        inv = inverse[0, h : h + 1, :]
        delta = jnp.sum(product[half], axis=0, keepdims=True) * inv
        high = delta.astype(BF16).astype(F32)
        mine = (row >= 64 * h) & (row < 64 * h + 64)
        scaled = jnp.where(mine, back * inv, 0.0)
        tail = jnp.where(row == 0, -high, jnp.where(row == 1, high - delta, 0.0))
        right = jnp.concatenate([scaled.astype(BF16), tail.astype(BF16)], axis=0)
        low = probs[h]
        score_back = low * dot(value, right).astype(BF16)
        query_parts.append((dot(key_t[half], score_back) * 0.125).astype(BF16))
        key_total += dot(score_back, jnp.where(mine, query, 0.0).T.astype(BF16))
        value_total += dot(low, scaled.T.astype(BF16))
    q_low = jnp.concatenate(query_parts, axis=0)
    k_low = key_total.astype(BF16)
    v_low = value_total.astype(BF16)
    query_back[pl.ds(pl.multiple_of(i * 128, 128), 128), :] = q_low
    pair = pl.ds(pl.multiple_of(i * 128, 128), 128)
    key_back[:, pair] = k_low
    value_back[:, pair] = v_low
    pieces = (4, 2, 2, 2, 16, 128)
    parts = (
        dot(normed_t[:, 0:ROWS], q_low, 1, 1),
        dot(normed_t[...], k_low),
        dot(normed_t[...], v_low),
    )
    for u, part in enumerate(parts):
        first_all[i, u] = part.astype(BF16).reshape(pieces)
        first_kept[i, u] = first_all[i, u, :, :, :, c]
    for k in range(4):
        pl.when(i == k)(lambda p=k: first_red.start(0, chunks[p]))

    @pl.when(i == 3)
    def _():
        gain, bias = vec_row(vec, 0, D), vec_row(vec, D, D)
        w_q, w_k, w_v = [w_first[u].reshape(D, D) for u in range(3)]
        normed, scale = normalize(text_t[...].astype(F32).T)
        text_back = dot(key_back[ROWS:KEYS], w_k, 1, 1) + dot(value_back[ROWS:KEYS], w_v, 1, 1)
        text_part[...] = (
            norm_back(text_back, gain, normed, scale).T.astype(BF16).reshape(8, 64, TEXT)
        )
        text_buf[w] = text_part[w]
        texts = "text", lambda: [
            (text_part.at[peer[0]], text_buf.at[w], peer) for peer in wide_peers(w, n)
        ]
        links.start(*texts)
        gain_grad = jnp.sum(text_back * normed, axis=0, keepdims=True)
        bias_grad = jnp.sum(text_back, axis=0, keepdims=True)

        step_rest(1, 3)
        step_first(2, 1)
        step_first(1, 3)
        step_first(3, 0)
        read[1].wait()
        read[2].wait()
        tile = ROWS // 2
        for t in range(2):
            rows = slice(t * tile, (t + 1) * tile)
            normed, scale = normalize(x_buf[rows].astype(F32))
            projected = (
                dot(query_back[:, rows], w_q, 0, 1)
                + dot(key_back[rows], w_k, 1, 1)
                + dot(value_back[rows], w_v, 1, 1)
            )
            patch_buf[rows] = middle_buf[rows] + norm_back(projected, gain, normed, scale)
            gain_grad = gain_grad + jnp.sum(projected * normed, axis=0, keepdims=True)
            bias_grad = bias_grad + jnp.sum(projected, axis=0, keepdims=True)
            if t == 0:
                step_first(2, 2)
                step_first(3, 1)
        write.start()
        for offset, piece in ((0, gain_grad), (4, bias_grad)):
            for r in range(4):
                v_own[offset + r : offset + r + 1, :] = piece[:, r * 128 : (r + 1) * 128]
        vw_buf[w] = v_own[...]
        wides = "wide", lambda: [(v_own, vw_buf.at[w], peer) for peer in wide_peers(w, n)]
        links.start(*wides)
        step_first(3, 2)
        step_rest(2, 3)
        step_first(2, 3)
        links.wait(*texts)
        total = text_buf[0].astype(F32)
        for k in range(1, 8):
            total = total + text_buf[k].astype(F32)
        text_out[...] = total
        links.wait(*wides)
        total = vw_buf[0]
        for k in range(1, 8):
            total = total + vw_buf[k]
        v_sum[...] = total
        vn_buf[n] = total
        narrows = "narrow", lambda: [(v_sum, vn_buf.at[n], peer) for peer in narrow_peers(w, n)]
        links.start(*narrows)
        owner, rank = unit_ranks(owners)
        step_first(3, 3)
        for q in range(4):
            for s in range(SLOTS):
                unit = jnp.int32(0)
                for u in range(UNITS):
                    unit = unit + jnp.where((owner[u] == q) & (rank[u] == s), u, 0)
                s_buf[q, s] = red[jnp.minimum(unit, UNITS - 1)]
        slots = "slots", lambda: [
            (s_buf.at[peer[1]], r_buf.at[n], peer) for peer in narrow_peers(w, n)
        ]
        links.start(*slots)
        r_buf[n] = s_buf[n]
        links.wait(*narrows)
        vec_out[...] = (vn_buf[0] + vn_buf[1]) + (vn_buf[2] + vn_buf[3])
        links.wait(*slots)
        for q in range(4):
            slot_grad[:, q * 16 : (q + 1) * 16, :] = r_buf[q].astype(F32)
        write.wait()


def back(
    owners, probs, inverse, keyed, v_t, back_t, q_t, att_t, normed_t, rest, w_first, text_t, x,
    middle_back, vec, vecs
):
    hbm = pl.BlockSpec(memory_space=pl.ANY)
    copies = 3 * 8 + 4 * 8 + 7 + 7 + 3 + 3
    bf = lambda *s: pltpu.VMEM(s, BF16)
    return pl.pallas_call(
        back_kernel,
        grid=(4,),
        in_specs=[
            smem(),
            pl.BlockSpec((2, KEYS, ROWS), lambda i: (i, 0, 0)),
            pl.BlockSpec((1, 2, ROWS), lambda i: (i, 0, 0)),
            pl.BlockSpec((None, KEYS, 128), lambda i: (i, 0, 0)),
            pl.BlockSpec((128, KEYS), lambda i: (i, 0)),
            pl.BlockSpec((128, ROWS), lambda i: (i, 0)),
            pl.BlockSpec((128, ROWS), lambda i: (i, 0)),
            pl.BlockSpec((128, ROWS), lambda i: (i, 0)),
            vmem(),
            hbm,
            vmem(),
            vmem(),
            hbm,
            hbm,
            vmem(),
        ]
        + [vmem()] * 4,
        out_specs=[hbm, vmem(), vmem(), vmem()],
        out_shape=[
            jax.ShapeDtypeStruct((ROWS, D), F32),
            jax.ShapeDtypeStruct((SLOTS, 64, D), F32),
            jax.ShapeDtypeStruct((64, TEXT), F32),
            jax.ShapeDtypeStruct((VEC // 128, 128), F32),
        ],
        scratch_shapes=[bf(9, 4, 2, 2, 16, D)]
        + reducer_scratch((9,), D)
        + reducer_scratch((4, 3), 128)
        + [
            bf(4, 3, 4, 2, 2, 2, 16, 128),
            bf(4, 3, 4, 2, 2, 16, 128),
            bf(UNITS, 16, D),
            bf(4, SLOTS, 16, D),
            bf(4, SLOTS, 16, D),
            bf(8, 64, TEXT),
            bf(8, 64, TEXT),
            pltpu.VMEM((VEC // 128, 128), F32),
            pltpu.VMEM((8, VEC // 128, 128), F32),
            pltpu.VMEM((VEC // 128, 128), F32),
            pltpu.VMEM((4, VEC // 128, 128), F32),
            bf(D, ROWS),
            bf(KEYS, D),
            bf(KEYS, D),
            bf(ROWS, D),
            pltpu.VMEM((ROWS, D), F32),
            pltpu.VMEM((ROWS, D), F32),
            pltpu.SemaphoreType.DMA((copies,)),
            pltpu.SemaphoreType.DMA((copies,)),
            pltpu.SemaphoreType.DMA((4,)),
        ],
        compiler_params=pltpu.CompilerParams(
            collective_id=2, has_side_effects=True, vmem_limit_bytes=63 * 2**20
        ),
    )(
        owners, probs, inverse, keyed, v_t, back_t, q_t, att_t, normed_t,
        rest.reshape(9, 4, 2, 2, 2, 16, D), w_first, text_t, x, middle_back, vec, *vecs,
    )


def reduce_all(owners, rest, first, text, vecs):
    vec = lax.psum(jnp.concatenate(vecs, axis=1), ("wide", "narrow"))
    text_sum = lax.psum_scatter(text.astype(F32), "wide", scatter_dimension=0, tiled=True)
    all_units = jnp.concatenate([first, rest], axis=0).astype(F32)
    rows = lax.psum_scatter(all_units, "wide", scatter_dimension=1, tiled=True)
    same = owners[:, None] == owners[None, :]
    ids = jnp.arange(UNITS)
    rank = jnp.sum((same & (ids[None, :] < ids[:, None])).astype(jnp.int32), axis=1)
    pick = (owners[None, None, :] == jnp.arange(lax.axis_size("narrow"))[:, None, None]) & (
        rank[None, None, :] == jnp.arange(SLOTS)[None, :, None]
    )
    terms = jnp.einsum("nsu,urc->nsrc", pick.astype(F32), rows, precision=lax.Precision.HIGHEST)
    slots = lax.psum_scatter(terms, "narrow", scatter_dimension=0, tiled=True)
    return slots[0], text_sum, vec.reshape(VEC // 128, 128)


def adam(master, moment_one, moment_two, averaged, gradient, rate):
    moment_one = beta_one * moment_one + (1.0 - beta_one) * gradient
    moment_two = beta_two * moment_two + (1.0 - beta_two) * gradient * gradient
    mean_hat = moment_one / (1.0 - beta_one**STEP)
    second_hat = moment_two / (1.0 - beta_two**STEP)
    master = master - rate * (
        mean_hat / (jnp.sqrt(second_hat) + adam_eps) + weight_decay * master
    )
    averaged = average_keep * averaged + (1.0 - average_keep) * master
    return master, moment_one, moment_two, averaged


def unit_rates():
    blocks = FF // D
    fans = [2 * D // 3, 2 * D // 3, D, D // 64] + [D] * blocks + [FF] * blocks
    return [float(fan) ** -0.5 for fan in fans]


def update_kernel(
    owners, grad, masters, first, second, average, text_t, vec_grad, vec, vec_first, vec_second,
    vec_average,
    new_masters, new_first, new_second, new_average, new_copies, text_grad,
    vec_new_value, vec_new_first, vec_new_second, vec_new_average,
):
    s = pl.program_id(0)
    n = lax.axis_index("narrow")
    owner, rank = unit_ranks(owners)
    rate, filled = jnp.float32(0.0), jnp.int32(0)
    for u, value in enumerate(unit_rates()):
        match = (owner[u] == n) & (rank[u] == s)
        rate = rate + jnp.where(match, jnp.float32(value), jnp.float32(0.0))
        filled = filled + match.astype(jnp.int32)
    state = adam(masters[0, 0], first[0, 0], second[0, 0], average[0, 0], grad[0], rate)
    keep = jnp.broadcast_to(filled, state[0].shape) > 0
    state = [jnp.where(keep, part, 0.0) for part in state]
    for ref, part in zip((new_masters, new_first, new_second, new_average), state):
        ref[0, 0] = part
    new_copies[0, 0] = state[0].astype(BF16)

    @pl.when(s == 0)
    def _():
        text_grad[0] = text_t[:, 0:LANG]
        state = adam(
            vec[...], vec_first[...], vec_second[...], vec_average[...], vec_grad[...], vector_rate
        )
        for ref, part in zip(
            (vec_new_value, vec_new_first, vec_new_second, vec_new_average), state
        ):
            ref[...] = part


def update(owners, grad, masters, first, second, average, text_t, vec_grad, vec, v1, v2, va):
    rows = masters.shape[2]
    state = jax.ShapeDtypeStruct(masters.shape, F32)
    vector = jax.ShapeDtypeStruct(vec.shape, F32)
    slot = pl.BlockSpec((1, 1, rows, D), lambda s: (0, s, 0, 0))
    vec_spec = pl.BlockSpec(vec.shape, lambda s: (0, 0))
    return pl.pallas_call(
        update_kernel,
        grid=(SLOTS,),
        out_shape=[state] * 4
        + [
            jax.ShapeDtypeStruct(masters.shape, BF16),
            jax.ShapeDtypeStruct((1, text_t.shape[0], LANG), F32),
        ]
        + [vector] * 4,
        in_specs=[smem(), pl.BlockSpec((1, rows, D), lambda s: (s, 0, 0))]
        + [slot] * 4
        + [pl.BlockSpec(text_t.shape, lambda s: (0, 0))]
        + [vec_spec] * 5,
        out_specs=[slot] * 5
        + [pl.BlockSpec((1, text_t.shape[0], LANG), lambda s: (0, 0, 0))]
        + [vec_spec] * 4,
        compiler_params=pltpu.CompilerParams(vmem_limit_bytes=VMEM_LIMIT),
    )(owners, grad, masters, first, second, average, text_t, vec_grad, vec, v1, v2, va)


def local(
    patches, text_tokens, view_counts, out_grad, owners, masters, first_moment, second_moment,
    average, vec_value, vec_first, vec_second, vec_average,
):
    vec, v1, v2, va = [
        part.reshape(VEC // 128, 128) for part in (vec_value, vec_first, vec_second, vec_average)
    ]
    text_in = jnp.swapaxes(text_tokens, 1, 2)
    if lax.axis_size("wide") == 8 and lax.axis_size("narrow") == 4:
        (att_t, probs, inverse, q_t, keyed, v_t, normed_t, w_first, w_rest, text_t) = front(
            owners, view_counts, masters, text_in, patches, vec
        )
        layer_out, middle_back, back_t, rest, *vecs = dense(
            view_counts, att_t, patches, out_grad, vec, w_rest.reshape(9, D, D)
        )
        patch_grad, slot_grad, text_sum, vec_grad = back(
            owners, probs, inverse, keyed, v_t, back_t, q_t, att_t, normed_t, rest, w_first,
            text_t.reshape(D, TEXT), patches, middle_back, vec, vecs,
        )
    else:
        units, text_t = gather(owners, masters, text_in)
        att_t, probs, inverse, q_t, keyed, v_t = attention_forward(
            view_counts, patches, text_t, vec, units
        )
        layer_out, middle_back, back_t, rest, *vecs = dense(
            view_counts, att_t, patches, out_grad, vec, units[3:]
        )
        query_back, key_back, value_back = attention_backward(
            probs, inverse, keyed, v_t, back_t, q_t, att_t
        )
        patch_grad, first, gain_one, bias_one, text_part = project_back(
            patches, text_t, vec, units, middle_back, query_back, key_back, value_back
        )
        slot_grad, text_sum, vec_grad = reduce_all(
            owners, rest, first, text_part, (gain_one, bias_one, *vecs)
        )
    outs = update(
        owners, slot_grad, masters, first_moment, second_moment, average, text_sum, vec_grad, vec,
        v1, v2, va,
    )
    new_masters, new_first, new_second, new_average, new_copies, text_grad = outs[:6]
    vectors = [part.reshape(VEC) for part in outs[6:]]
    return (
        layer_out, patch_grad, jnp.swapaxes(text_grad, 1, 2), new_masters, new_first, new_second,
        new_average, new_copies, *vectors,
    )


def solution(mesh):
    rows = P(("wide", "narrow"), None)
    state = P("narrow", None, "wide", None)
    text = P("narrow", None, "wide")
    in_specs = (rows, text, rows, rows, P(), state, state, state, state, P(), P(), P(), P())
    out_specs = (rows, rows, text, state, state, state, state, state, P(), P(), P(), P())
    return jax.shard_map(local, mesh=mesh, in_specs=in_specs, out_specs=out_specs, check_vma=False)
```

time: 237 us -> 190 us (0.80); the launches traced: 236 us -> 187 us
  Pallas kernels: 224 us -> 184 us
  other arithmetic: 5.49 us -> 0 us
  local copies, waits for them, and re-layouts: 6.13 us -> 1.5 us
    pallas_call x6 -> x3, Pallas kernels: 191 us -> 151 us  [the longest x1 83.4 us: back(): pl.pallas_call(back_kernel, grid=(4,), in_specs=[smem(), pl.BlockSpec((2,...]
    pallas_call x4 -> x0, other arithmetic: 5.49 us -> none  [update(): pl.pallas_call(update_kernel, out_shape=[state] * 4 + [jax.ShapeDtypeStru...]
    reshape x4 -> x0, local copies, waits for them, and re-layouts: 3.21 us -> none  [the longest x1 1.35 us: local(): vec = vec_value.reshape(1, VEC)]
where the time goes in v2:
time: 190 us; the launch traced here: 187 us
  Pallas kernels  184 us (97%)
    pallas_call x1, Pallas kernels, back(): pl.pallas_call(back_kernel, grid=(4,), in_specs=[smem(), pl.BlockSpec((2,...  83.4 us
    pallas_call x1, Pallas kernels, front(): pl.pallas_call(front_kernel, grid=(4,), in_specs=[smem(), smem(), vmem(),...  63.2 us
    pallas_call x1, Pallas kernels, dense(): pl.pallas_call(functools.partial(dense_kernel, tile=tile), grid=(ROWS //...  33.2 us
    pallas_call x1, Pallas kernels, update(): pl.pallas_call(update_kernel, grid=(SLOTS,), out_shape=[state] * 4 + [jax...  4.57 us

profile of v2, /device:TPU:0, one launch (start us, length us, event | category | flops | bytes accessed | tf_op | source)
XLA Modules:
  0.0 186.8 jit_solution(8135454850915601213)
XLA Ops:
  0.6 63.2 %shard_map.220 = (bf16[512,1280]{1,0:T(8,128)(2,1)}, bf16[8,1408,1280]{2,1,0:T(8,128)(2,1)}, f32[4,2,1280]{2,1,0:T(2,128)}, bf16[512,1280]{1,0:T(8,128)(2,1)}, b...) custom-call(s32[12]{0:T(128)} %owners.5, ...), custom_call_target="tpu_custom_call" | custom-call | tf_op jit(solution)/shard_map/pallas_call | solution.py:317
  63.9 33.2 %shard_map.221 = (bf16[1280,512]{1,0:T(8,128)(2,1)}, f32[1280,512]{1,0:T(8,128)}, bf16[512,1280]{1,0:T(8,128)(2,1)}, bf16[9,512,512]{2,1,0:T(8,128)(2,1)}, f32[1...) custom-call(s32[1,5]{1,0:T(1,128)} %counts.3, ...), custom_call_target="tpu_custom_call" | custom-call | tf_op jit(solution)/shard_map/pallas_call | solution.py:509
  97.1 83.4 %shard_map.222 = (f32[1280,512]{1,0:T(8,128)}, f32[4,64,512]{2,1,0:T(8,128)}, f32[64,128]{1,0:T(8,128)}, f32[36,128]{1,0:T(8,128)}) custom-call(s32[12]{0:T(128)} %owners.5, bf16[8,1408,1280]{2,1,0:T(8,128)(2,1)} %get-tuple-element.47.probs, f32[4,2,1280]{2,1,0:T(2,128)} %get-tuple-element.48.inverse, bf16[4,1408,128]{2,1,0:T(8,128)(2,1)} %get-tuple-element.49.keyed, ...), custom_call_target="tpu_custom_call" | custom-call | tf_op jit(solution)/shard_map/pallas_call | solution.py:943
  180.6 0.0 copy-start
  180.6 4.6 %shard_map.223 = (f32[1,4,64,512]{3,2,1,0:T(8,128)}, f32[1,4,64,512]{3,2,1,0:T(8,128)}, f32[1,4,64,512]{3,2,1,0:T(8,128)}, f32[1,4,64,512]{3,2,1,0:T(8,128)}, bf...) custom-call(s32[12]{0:T(128)} %owners.5, ...), custom_call_target="tpu_custom_call" | custom-call | tf_op jit(solution)/shard_map/pallas_call | solution.py:1078
  185.1 0.0 copy-done
  185.2 1.5 copy.26
Async XLA Ops:
  180.6 4.6 %copy-start = (f32[1280,512]{1,0:T(8,128)S(1)}, f32[1280,512]{1,0:T(8,128)}, u32[]{:S(2)}) copy-start(f32[1280,512]{1,0:T(8,128)} %get-tuple-element.89) | copy-start | bytes 7864324
